TPU v7x, 32 devices: a whole 2x2x4 slice. The times are simulated.
32 devices in a mesh: rep: 16 (over z, x, core), shard: 2 (over y).
Axes of the slice: x: 2, y: 2, z: 4, core: 2. Of those that a mesh axis runs over, the one named last changes fastest.
Arguments:
- layer_input: bfloat16 [32768, 576], P(('rep', 'shard')), may hold values from -6 to 6
- seq_lengths: int32 [128], P(('rep', 'shard')), may hold values from 0 to 1024, as said below
- out_cotangent: bfloat16 [32768, 576], P(('rep', 'shard')), may hold values from -6 to 6
- attn_gain: bfloat16 [576], P('shard'), may hold values from 0.099609375 to 1.8984375
- w_query: bfloat16 [576, 576], P('shard'), may hold values from -0.25 to 0.25
- w_key: bfloat16 [576, 192], P('shard'), may hold values from -0.25 to 0.25
- w_value: bfloat16 [576, 192], P('shard'), may hold values from -0.25 to 0.25
- w_out: bfloat16 [576, 576], P('shard'), may hold values from -1.5 to 1.5
- mlp_gain: bfloat16 [576], P('shard'), may hold values from 0.099609375 to 1.8984375
- w_gate: bfloat16 [576, 1536], P('shard'), may hold values from -0.25 to 0.25
- w_up: bfloat16 [576, 1536], P('shard'), may hold values from -0.25 to 0.25
- w_down: bfloat16 [1536, 576], P('shard'), may hold values from -0.15625 to 0.15625
Outputs:
- layer_output: bfloat16 [32768, 576], P(('rep', 'shard'))
- input_grad: bfloat16 [32768, 576], P(('rep', 'shard'))
- attn_gain_grad: float32 [576], P('shard')
- w_query_grad: float32 [576, 576], P('shard')
- w_key_grad: float32 [576, 192], P('shard')
- w_value_grad: float32 [576, 192], P('shard')
- w_out_grad: float32 [576, 576], P('shard')
- mlp_gain_grad: float32 [576], P('shard')
- w_gate_grad: float32 [576, 1536], P('shard')
- w_up_grad: float32 [576, 1536], P('shard')
- w_down_grad: float32 [1536, 576], P('shard')
Inputs may be any that keep to these rules, and one draw needn't show every extreme that they name: `seq_lengths`: each run of 4 entries belongs to one device. A length of 0 is an empty slot. On every device the sum over its slots of ceil(length / 128) is at most 8, and at least 4. Some device holds one sequence of exactly 1024 tokens.
All inputs are finite; a program needn't handle non-finite values.
Results may differ from a plain program's by a relative error of at most 0.02.
Values may be sent and summed in bfloat16 or wider, within the bound.
A program may use at most 128 MiB of HBM per device.

v0:
```python
import functools

import jax
import jax.numpy as jnp
from jax import lax
from jax.experimental import pallas as pl
from jax.experimental.pallas import tpu as pltpu
from jax.sharding import PartitionSpec as P

HEADS = 9
KV_HEADS = 3
HEAD_DIM = 64
PAD_BLOCK = 128


norm_eps = 1e-05
rope_theta = 100000.0
masked_score = -1e30


def layout(length_row, total_rows):
    block_count = (length_row + PAD_BLOCK - 1) // PAD_BLOCK
    stop_rows = jnp.cumsum(block_count) * PAD_BLOCK
    first_rows = stop_rows - block_count * PAD_BLOCK
    row_index = jnp.arange(total_rows, dtype=jnp.int32)
    inside = (row_index[:, None] >= first_rows[None, :]) & (
        row_index[:, None] < (first_rows + length_row)[None, :]
    )
    slot_ids = jnp.arange(length_row.shape[0], dtype=jnp.int32)
    live_rows = jnp.any(inside, axis=1)
    slot_of_row = jnp.sum(jnp.where(inside, slot_ids[None, :], 0), axis=1)
    labels = jnp.where(live_rows, slot_of_row, -1)
    offsets = jnp.sum(jnp.where(inside, row_index[:, None] - first_rows[None, :], 0), axis=1)
    return (labels, live_rows, offsets)


def rotary_tables(offsets):
    half_dim = HEAD_DIM // 2
    exponent = jnp.arange(half_dim, dtype=jnp.float32) * (2.0 / HEAD_DIM)
    frequency = jnp.power(jnp.float32(rope_theta), -exponent)
    angles = offsets.astype(jnp.float32)[:, None] * frequency[None, :]
    return (jnp.cos(angles), jnp.sin(angles))

GROUP = HEADS // KV_HEADS
ATT_BLOCK = 256
F32 = jnp.float32
BF16 = jnp.bfloat16


def dot(left, right, left_dim=1, right_dim=0):
    return lax.dot_general(
        left, right, (((left_dim,), (right_dim,)), ((), ())), preferred_element_type=F32
    )


def swap_halves(rows):
    half = HEAD_DIM // 2
    return jnp.concatenate([rows[:, half:], rows[:, :half]], axis=1)


def unit_and_scale(rows):
    scale = lax.rsqrt(jnp.mean(rows * rows, axis=1, keepdims=True) + norm_eps)
    return rows * scale, scale


def allowed_block(label_col, label_row, begin, size):
    keys = begin + size
    shape = (size, keys)
    row = begin + lax.broadcasted_iota(jnp.int32, shape, 0)
    col = lax.broadcasted_iota(jnp.int32, shape, 1)
    return (label_col[begin:keys, :] == label_row[:, :keys]) & (col <= row)


def forward_kernel(
    x_ref, gain_ref, wqkv_ref, wout_ref, cos_ref, sin_ref, lcol_ref, lrow_ref,
    q_ref, k_ref, v_ref, att_ref, lse_ref, mid_ref, n1_ref,
):
    rows = x_ref.shape[0]

    @pl.when(pl.program_id(0) == 0)
    def _():
        x = x_ref[...].astype(F32)
        unit, _ = unit_and_scale(x)
        n1_ref[...] = (unit * gain_ref[...].astype(F32)).astype(BF16)
        mid_ref[...] = x

    proj = dot(n1_ref[...], wqkv_ref[0])
    cos, sin = cos_ref[...], sin_ref[...]
    for head in range(GROUP + 1):
        part = proj[:, head * HEAD_DIM : (head + 1) * HEAD_DIM]
        turned = part * cos + swap_halves(part) * sin
        if head < GROUP:
            q_ref[0, head] = (turned * (HEAD_DIM ** -0.5)).astype(BF16)
        else:
            k_ref[0] = turned.astype(BF16)
    v_ref[0] = proj[:, (GROUP + 1) * HEAD_DIM :].astype(BF16)
    for begin in range(0, rows, ATT_BLOCK):
        stop = begin + ATT_BLOCK
        allowed = allowed_block(lcol_ref, lrow_ref, begin, ATT_BLOCK)
        keys, values = k_ref[0, :stop, :], v_ref[0, :stop, :]
        for head in range(GROUP):
            scores = dot(q_ref[0, head, begin:stop, :], keys, 1, 1)
            scores = jnp.where(allowed, scores, masked_score)
            top = jnp.max(scores, axis=1, keepdims=True)
            weights = jnp.exp(scores - top)
            total = jnp.sum(weights, axis=1, keepdims=True)
            low = (weights * (1.0 / total)).astype(BF16)
            mixed = dot(low, values)
            att_ref[0, begin:stop, head * HEAD_DIM : (head + 1) * HEAD_DIM] = mixed.astype(BF16)
            lse_ref[0, begin:stop, head : head + 1] = top + jnp.log(total)
    mid_ref[...] += dot(att_ref[0], wout_ref[...])


def mlp_kernel(
    mid_ref, cot_ref, live_ref, gain_ref, wg_ref, wu_ref, wd_ref, att_ref,
    out_ref, gm_ref, ga_ref, gb_ref, gain_grad_ref,
    n2_ref, low_ref, acc_ref, gn_ref,
):
    step = pl.program_id(0)

    @pl.when(step == 0)
    def _():
        unit, _ = unit_and_scale(mid_ref[...])
        n2_ref[...] = (unit * gain_ref[...].astype(F32)).astype(BF16)
        low_ref[...] = jnp.where(live_ref[...] > 0, cot_ref[...].astype(F32), 0.0).astype(BF16)
        acc_ref[...] = mid_ref[...]
        gn_ref[...] = jnp.zeros_like(gn_ref)

    n2, low = n2_ref[...], low_ref[...]
    gate = dot(n2, wg_ref[...])
    up = dot(n2, wu_ref[...])
    hidden_grad = dot(low, wd_ref[...], 1, 1)
    sig = jax.nn.sigmoid(gate)
    silu = gate * sig
    hidden = (silu * up).astype(BF16)
    up_grad = (hidden_grad * silu).astype(BF16)
    gate_grad = (hidden_grad * up * sig * (1.0 + gate * (1.0 - sig))).astype(BF16)
    acc_ref[...] += dot(hidden, wd_ref[...])
    gn_ref[...] += dot(gate_grad, wg_ref[...], 1, 1) + dot(up_grad, wu_ref[...], 1, 1)
    rows, lanes = ga_ref.shape[2] // 2, ga_ref.shape[3]
    gate_w = dot(n2, gate_grad, 0, 0).astype(BF16)
    up_w = dot(n2, up_grad, 0, 0).astype(BF16)
    for part in range(2):
        for shard in range(2):
            at = (slice(shard * rows, (shard + 1) * rows), slice(part * lanes, (part + 1) * lanes))
            ga_ref[2 * step + part, shard, :rows, :] = gate_w[at]
            ga_ref[2 * step + part, shard, rows:, :] = up_w[at]
    down_w = dot(hidden, low, 0, 0).astype(BF16)
    size = down_w.shape[0] // 4
    for part in range(4):
        block = down_w[part * size : (part + 1) * size]
        gb_ref[part, step, :size, :] = block[:, :lanes]
        gb_ref[part, step, size : size + size // 2, : lanes // 2] = block[: size // 2, lanes:]
        gb_ref[part, step, size : size + size // 2, lanes // 2 :] = block[size // 2 :, lanes:]

    @pl.when(step == pl.num_programs(0) - 1)
    def _():
        live = live_ref[...] > 0
        out_ref[...] = jnp.where(live, acc_ref[...], 0.0).astype(BF16)
        unit, scale = unit_and_scale(mid_ref[...])
        grad = gn_ref[...]
        gain_grad_ref[...] = jnp.sum(grad * unit, axis=0, keepdims=True)
        scaled = grad * gain_ref[...].astype(F32)
        gm = low_ref[...].astype(F32) + scale * (
            scaled - unit * jnp.mean(scaled * unit, axis=1, keepdims=True)
        )
        gm_ref[...] = gm
        gm_low = gm.astype(BF16)
        grads = [dot(att_ref[group], gm_low, 0, 0) for group in range(KV_HEADS)]
        grads = jnp.concatenate(grads, axis=0)
        piece = grads.shape[0] // 8
        base = size + size // 2
        extra = jnp.zeros((8, grads.shape[1]), F32)
        side = jnp.zeros((piece + 8, 2 * lanes - grads.shape[1]), F32)
        for shard in range(2):
            for part in range(4):
                at = (shard * 4 + part) * piece
                block = jnp.concatenate([grads[at : at + piece], extra], axis=0)
                wide = jnp.concatenate([block[:, lanes:], side], axis=1)
                gb_ref[part, shard, base : base + piece + 8, :] = block[:, :lanes].astype(BF16)
                gb_ref[part, shard, base + piece + 8 :, :] = wide.astype(BF16)


def backward_kernel(
    first, last, x_ref, gain_ref, gm_ref, q_ref, k_ref, v_ref, lse_ref, wqkv_ref, wout_ref,
    cos_ref, sin_ref, lcol_ref, lrow_ref, gain_two_ref, gn_in_ref, after_a_ref, after_b_ref,
    xg_ref, gw_ref,
    n1_ref, low_ref, gn_ref, cat_ref, dk_ref, dv_ref,
):
    rows = x_ref.shape[0]
    unit, scale = unit_and_scale(x_ref[...].astype(F32))
    n1_ref[...] = (unit * gain_ref[...].astype(F32)).astype(BF16)
    low_ref[...] = gm_ref[...].astype(BF16)
    dk_ref[...] = jnp.zeros_like(dk_ref)
    dv_ref[...] = jnp.zeros_like(dv_ref)
    att_grad = dot(low_ref[...], wout_ref[...], 1, 1).astype(BF16)
    for begin in range(0, rows, ATT_BLOCK):
        stop = begin + ATT_BLOCK
        allowed = allowed_block(lcol_ref, lrow_ref, begin, ATT_BLOCK)
        keys, values = k_ref[0, :stop, :], v_ref[0, :stop, :]
        cos, sin = cos_ref[begin:stop, :], sin_ref[begin:stop, :]
        for head in range(GROUP):
            queries = q_ref[0, head, begin:stop, :]
            grads = att_grad[begin:stop, head * HEAD_DIM : (head + 1) * HEAD_DIM]
            scores = jnp.where(allowed, dot(queries, keys, 1, 1), masked_score)
            weights = jnp.exp(scores - lse_ref[0, begin:stop, head : head + 1])
            weight_grad = dot(grads, values, 1, 1)
            centre = jnp.sum(weights * weight_grad, axis=1, keepdims=True)
            score_grad = (weights * (weight_grad - centre)).astype(BF16)
            dk_ref[:stop, :] += dot(score_grad, queries, 0, 0)
            dv_ref[:stop, :] += dot(weights.astype(BF16), grads, 0, 0)
            dq = dot(score_grad, keys) * (HEAD_DIM ** -0.5)
            cat_ref[begin:stop, head * HEAD_DIM : (head + 1) * HEAD_DIM] = (
                dq * cos - swap_halves(dq) * sin
            ).astype(BF16)
    dk = dk_ref[...]
    cat_ref[:, GROUP * HEAD_DIM : (GROUP + 1) * HEAD_DIM] = (
        dk * cos_ref[...] - swap_halves(dk) * sin_ref[...]
    ).astype(BF16)
    cat_ref[:, (GROUP + 1) * HEAD_DIM :] = dv_ref[...].astype(BF16)
    gn_ref[...] = dot(cat_ref[...], wqkv_ref[0], 1, 1)
    if not first:
        gn_ref[...] += gn_in_ref[...]
    grad_w = dot(n1_ref[...], cat_ref[...], 0, 0)
    piece = grad_w.shape[0] // 8
    half = piece * 4
    for shard in range(2):
        tail = jnp.zeros((8, grad_w.shape[1]), F32)
        if last:
            grad = gn_ref[...]
            unit, scale = unit_and_scale(x_ref[...].astype(F32))
            cut = slice(shard * half, (shard + 1) * half)
            gain_sum = jnp.sum(grad * unit, axis=0, keepdims=True)
            tail = jnp.concatenate(
                [gain_sum[:, cut], gain_two_ref[:, cut], jnp.zeros((6, half), F32)], axis=0
            )
            tail = jnp.concatenate([tail, jnp.zeros((8, grad_w.shape[1] - half), F32)], axis=1)
        for part in range(4):
            at = (shard * 4 + part) * piece
            block = jnp.concatenate([grad_w[at : at + piece], tail], axis=0)
            gw_ref[part, shard] = block.astype(BF16)
    if last:
        unit, scale = unit_and_scale(x_ref[...].astype(F32))
        scaled = gn_ref[...] * gain_ref[...].astype(F32)
        xg_ref[...] = (
            gm_ref[...]
            + scale * (scaled - unit * jnp.mean(scaled * unit, axis=1, keepdims=True))
        ).astype(BF16)
    else:
        xg_ref[...] = gn_ref[...]


def assemble_kernel(shard_ref, q_ref, k_ref, v_ref, o_ref, far_ref, qkv_ref, out_ref):
    rows = q_ref.shape[0]
    shard = shard_ref[0]
    starts = (0, q_ref.shape[1], q_ref.shape[1] + k_ref.shape[1])
    starts = starts + (starts[2] + v_ref.shape[1],)

    def put(at, parts, out):
        where = slice(at * rows, (at + 1) * rows)
        out_ref[where, :] = out
        for group in range(KV_HEADS):
            begin = 0
            for part, size in zip(parts, (GROUP * HEAD_DIM, HEAD_DIM, HEAD_DIM)):
                qkv_ref[group, where, begin : begin + size] = part[
                    :, group * size : (group + 1) * size
                ]
                begin += size

    for near in range(2):

        @pl.when(shard == near)
        def _():
            put(near, (q_ref[...], k_ref[...], v_ref[...]), o_ref[...])
            far = far_ref[...]
            pieces = tuple(far[:, starts[i] : starts[i + 1]] for i in range(3))
            put(1 - near, pieces, far[:, starts[3] :])


def whole(shape):
    return pl.BlockSpec(shape, lambda i: (0,) * len(shape))


def lead(shape):
    return pl.BlockSpec(shape, lambda i: (i,) + (0,) * (len(shape) - 1))


def params(**more):
    return pltpu.CompilerParams(vmem_limit_bytes=60 * 1024 * 1024, **more)


def take(array, index, axis=0):
    return lax.dynamic_index_in_dim(array, index, axis, keepdims=False)


def swap(array, axis, size, bit):
    return lax.ppermute(array, axis, [(i, i ^ bit) for i in range(size)])


def halve(array, axis, size, bit, mine):
    sent = swap(take(array, 1 - mine), axis, size, bit)
    return (take(array, mine).astype(F32) + sent.astype(F32)).astype(BF16)


def both(array, other, mine):
    return jnp.where(mine == 0, jnp.stack([array, other]), jnp.stack([other, array]))


def reduce_steps(array, core, x, shard, n_rep, shard_first):
    array = halve(array, "rep", n_rep, 1, core)
    yield array
    if shard_first:
        array = halve(jnp.swapaxes(array, 0, 1), "shard", 2, 1, shard)
        yield array
        array = halve(array, "rep", n_rep, 2, x)
    else:
        array = halve(array, "rep", n_rep, 2, x)
        yield array
        array = halve(array, "shard", 2, 1, shard)
    yield array
    bit = 4
    while bit < n_rep:
        array = (array.astype(F32) + swap(array, "rep", n_rep, bit).astype(F32)).astype(BF16)
        bit *= 2
    array = both(array, swap(array, "rep", n_rep, 2), x)
    array = both(array, swap(array, "rep", n_rep, 1), core)
    yield array.reshape((4,) + array.shape[2:])


def gather_halves(first, second, core, shard, n_rep):
    got = swap(jnp.where(core == 0, first, second), "shard", 2, 1)
    other = swap(got, "rep", n_rep, 1)
    far_first = jnp.where(core == 0, got, other)
    far_second = jnp.where(core == 0, other, got)

    def join(near, far):
        return both(near, far, shard).reshape((-1,) + near.shape[1:])

    return join(first, far_first), join(second, far_second)


def local(
    n_rep, n_shard, layer_input, seq_lengths, out_cotangent, attn_gain, w_query, w_key, w_value,
    w_out, mlp_gain, w_gate, w_up, w_down,
):
    rows, width = layer_input.shape
    ff = w_gate.shape[1]
    group_width = GROUP * HEAD_DIM
    packed_width = group_width + 2 * HEAD_DIM
    quick = n_shard == 2 and n_rep >= 4 and n_rep & (n_rep - 1) == 0
    rep, shard = lax.axis_index("rep"), lax.axis_index("shard")
    core, x_bit = rep % 2, (rep // 2) % 2

    own_rows = w_query.shape[0]
    if quick:
        pack = jnp.concatenate([w_query, w_key, w_value, w_out], axis=1)
        far = swap(pack, "shard", 2, 1)
        gains = jnp.stack([attn_gain, mlp_gain])
        far_gains = swap(gains, "shard", 2, 1)
        gains = both(gains, far_gains, shard).swapaxes(0, 1).reshape(2, width)
        gain_one, gain_two = gains[:1], gains[1:]
        qkv_full, out_full = pl.pallas_call(
            assemble_kernel,
            in_specs=[pl.BlockSpec(memory_space=pltpu.SMEM)]
            + [pl.BlockSpec(memory_space=pltpu.VMEM)] * 5,
            out_specs=[pl.BlockSpec(memory_space=pltpu.VMEM)] * 2,
            out_shape=[
                jax.ShapeDtypeStruct((KV_HEADS, width, packed_width), BF16),
                jax.ShapeDtypeStruct((width, width), BF16),
            ],
            compiler_params=params(),
            name="assemble",
        )(shard[None], w_query, w_key, w_value, w_out, far)
        gate_full, up_full = gather_halves(w_gate, w_up, core, shard, n_rep)
        down_half = w_down.shape[0] // 2
        top, low = gather_halves(w_down[:down_half], w_down[down_half:], core, shard, n_rep)
        down_full = jnp.concatenate(
            [top.reshape(2, down_half, width), low.reshape(2, down_half, width)], axis=1
        ).reshape(-1, width)
    else:
        gather = functools.partial(lax.all_gather, axis_name="shard", axis=0, tiled=True)
        qkv = jnp.concatenate(
            [
                w_query.reshape(own_rows, KV_HEADS, group_width),
                w_key.reshape(own_rows, KV_HEADS, HEAD_DIM),
                w_value.reshape(own_rows, KV_HEADS, HEAD_DIM),
            ],
            axis=2,
        ).reshape(own_rows, -1)
        qkv_full, out_full = gather(qkv), gather(w_out)
        qkv_full = qkv_full.reshape(width, KV_HEADS, packed_width).swapaxes(0, 1)
        gate_full, up_full, down_full = gather(w_gate), gather(w_up), gather(w_down)
        gain_one, gain_two = gather(attn_gain)[None], gather(mlp_gain)[None]

    labels, live_rows, offsets = layout(seq_lengths, rows)
    cosine, sine = rotary_tables(offsets)
    cos_full = jnp.concatenate([cosine, cosine], axis=1)
    sin_full = jnp.concatenate([-sine, sine], axis=1)
    label_col, label_row = labels[:, None], labels[None, :]
    live = live_rows.astype(F32)[:, None]

    shape = jax.ShapeDtypeStruct
    head_block = lead((1, GROUP, rows, HEAD_DIM))
    kv_block = lead((1, rows, HEAD_DIM))
    lse_block = lead((1, rows, GROUP))
    qkv_block = lead((1, width, packed_width))
    out_block = lead((group_width, width))
    tables = [whole((rows, HEAD_DIM))] * 2 + [whole((rows, 1)), whole((1, rows))]
    row_block, gain_block = whole((rows, width)), whole((1, width))
    queries, keys, values, attended, lse, middle = pl.pallas_call(
        forward_kernel,
        grid=(KV_HEADS,),
        in_specs=[row_block, gain_block, qkv_block, out_block] + tables,
        out_specs=[
            head_block, kv_block, kv_block, lead((1, rows, group_width)), lse_block, row_block,
        ],
        out_shape=[
            shape((KV_HEADS, GROUP, rows, HEAD_DIM), BF16),
            shape((KV_HEADS, rows, HEAD_DIM), BF16),
            shape((KV_HEADS, rows, HEAD_DIM), BF16),
            shape((KV_HEADS, rows, group_width), BF16),
            shape((KV_HEADS, rows, GROUP), F32),
            shape((rows, width), F32),
        ],
        scratch_shapes=[pltpu.VMEM((rows, width), BF16)],
        compiler_params=params(),
        cost_estimate=pl.CostEstimate(
            flops=30_000_000_000, bytes_accessed=20_000_000, transcendentals=6_000_000
        ),
        name="attention_forward",
    )(layer_input, gain_one, qkv_full, out_full, cos_full, sin_full, label_col, label_row)

    steps, parts = 2, 4
    chunk, per_step = ff // steps, parts // steps
    lanes = ff // parts
    piece, half = width // 8, width // 2
    b_rows = ff // 8 + ff // 16 + 2 * (piece + 8)
    layer_output, gm, g_a, g_b, g_gain = pl.pallas_call(
        mlp_kernel,
        grid=(steps,),
        in_specs=[
            row_block, row_block, whole((rows, 1)), gain_block,
            pl.BlockSpec((width, chunk), lambda i: (0, i)),
            pl.BlockSpec((width, chunk), lambda i: (0, i)),
            lead((chunk, width)),
            whole((KV_HEADS, rows, group_width)),
        ],
        out_specs=[
            row_block, row_block,
            whole((parts, 2, width, lanes)),
            whole((parts, 2, b_rows, lanes)),
            gain_block,
        ],
        out_shape=[
            shape((rows, width), BF16),
            shape((rows, width), F32),
            shape((parts, 2, width, lanes), BF16),
            shape((parts, 2, b_rows, lanes), BF16),
            shape((1, width), F32),
        ],
        scratch_shapes=[
            pltpu.VMEM((rows, width), BF16),
            pltpu.VMEM((rows, width), BF16),
            pltpu.VMEM((rows, width), F32),
            pltpu.VMEM((rows, width), F32),
        ],
        compiler_params=params(),
        cost_estimate=pl.CostEstimate(
            flops=30_000_000_000, bytes_accessed=20_000_000, transcendentals=2_000_000
        ),
        name="mlp_both",
    )(middle, out_cotangent, live, gain_two, gate_full, up_full, down_full, attended)

    padded = piece + 8
    g_parts = []
    carried = jnp.zeros((8, 128), F32)

    def steps_of(array, shard_first):
        array = array.reshape((2, 2) + array.shape[1:])
        return reduce_steps(array, core, x_bit, shard, n_rep, shard_first)

    if quick:
        steps_a, steps_b = steps_of(g_a, True), steps_of(g_b, False)
    after = (jnp.zeros((8, 128), BF16),) * 2
    for group in range(KV_HEADS):
        first, last = group == 0, group == KV_HEADS - 1

        def at_group(block, group=group):
            return pl.BlockSpec(block, lambda i: (group,) + (0,) * (len(block) - 1))

        carried, g_part = pl.pallas_call(
            functools.partial(backward_kernel, first, last),
            grid=(1,),
            in_specs=[
                row_block, gain_block, row_block,
                at_group((1, GROUP, rows, HEAD_DIM)), at_group((1, rows, HEAD_DIM)),
                at_group((1, rows, HEAD_DIM)), at_group((1, rows, GROUP)),
                at_group((1, width, packed_width)), at_group((group_width, width)),
            ] + tables + [gain_block, whole(carried.shape)]
            + [pl.BlockSpec(memory_space=pl.ANY)] * 2,
            out_specs=[row_block, whole((4, 2, padded, packed_width))],
            out_shape=[
                shape((rows, width), BF16 if last else F32),
                shape((4, 2, padded, packed_width), BF16),
            ],
            scratch_shapes=[
                pltpu.VMEM((rows, width), BF16),
                pltpu.VMEM((rows, width), BF16),
                pltpu.VMEM((rows, width), F32),
                pltpu.VMEM((rows, packed_width), BF16),
                pltpu.VMEM((rows, HEAD_DIM), F32),
                pltpu.VMEM((rows, HEAD_DIM), F32),
            ],
            compiler_params=params(),
            cost_estimate=pl.CostEstimate(
                flops=15_000_000_000, bytes_accessed=12_000_000, transcendentals=2_000_000
            ),
            name="attention_backward",
        )(
            layer_input, gain_one, gm, queries, keys, values, lse, qkv_full, out_full,
            cos_full, sin_full, label_col, label_row, g_gain, carried, *after,
        )
        if quick:
            after = (next(steps_a), next(steps_b))
        g_parts.append(g_part)
    input_grad = carried
    g_qkv = jnp.stack(g_parts, axis=2)

    def columns(array):
        array = jnp.moveaxis(array, 0, -2)
        return array.reshape(-1, ff)

    def unfold(array):
        cut = ff // 8
        left, right = array[..., :cut, :], array[..., cut : cut + cut // 2, :]
        right = jnp.concatenate([right[..., : lanes // 2], right[..., lanes // 2 :]], axis=-2)
        down = jnp.concatenate([left, right], axis=-1)
        at = cut + cut // 2
        left = array[..., at : at + piece, :]
        right = array[..., at + piece + 8 : at + 2 * piece + 8, : width - lanes]
        return down, jnp.concatenate([left, right], axis=-1)

    if quick:
        *_, got = steps_of(g_qkv, True)
        b_own, a_own = next(steps_b), next(steps_a)
        gate_final, up_final = columns(a_own[:, :half]), columns(a_own[:, half:])
        down_own, out_own = unfold(b_own)
        down_final, out_final = down_own.reshape(-1, width), out_own.reshape(-1, width)
        gain_rows = got[0, KV_HEADS - 1, piece : piece + 2, :half]
        gain_one_final, gain_two_final = gain_rows[0], gain_rows[1]
        qkv_grad = got[:, :, :piece].swapaxes(1, 2).reshape(half, KV_HEADS, packed_width)
    else:
        def sums(array):
            owned = lax.psum_scatter(array, "shard", scatter_dimension=0, tiled=True)
            return lax.psum(owned, "rep")

        gate_final, up_final = sums(columns(g_a[:, :, :half])), sums(columns(g_a[:, :, half:]))
        down_all, out_all = unfold(jnp.swapaxes(g_b, 0, 1))
        down_final, out_final = sums(down_all.reshape(ff, width)), sums(out_all.reshape(width, width))
        gain_rows = g_qkv[0, :, KV_HEADS - 1, piece : piece + 2, :half]
        gain_one_final = sums(gain_rows[:, 0].reshape(width))
        gain_two_final = sums(gain_rows[:, 1].reshape(width))
        qkv_grad = g_qkv[:, :, :, :piece].transpose(1, 0, 3, 2, 4)
        qkv_grad = sums(qkv_grad.reshape(width, KV_HEADS, packed_width))
    own = qkv_grad.shape[0]
    query_final = qkv_grad[:, :, :group_width].reshape(own, -1)
    key_final = qkv_grad[:, :, group_width : group_width + HEAD_DIM].reshape(own, -1)
    value_final = qkv_grad[:, :, group_width + HEAD_DIM :].reshape(own, -1)
    finals = (
        gain_one_final, query_final, key_final, value_final, out_final,
        gain_two_final, gate_final, up_final, down_final,
    )
    return (layer_output, input_grad) + tuple(final.astype(F32) for final in finals)


def solution(mesh):
    return jax.shard_map(
        functools.partial(local, mesh.shape["rep"], mesh.shape["shard"]),
        mesh=mesh,
        in_specs=(
            P(("rep", "shard"), None),
            P(("rep", "shard")),
            P(("rep", "shard"), None),
            P("shard"),
            P("shard", None),
            P("shard", None),
            P("shard", None),
            P("shard", None),
            P("shard"),
            P("shard", None),
            P("shard", None),
            P("shard", None),
        ),
        out_specs=(
            P(("rep", "shard"), None),
            P(("rep", "shard"), None),
            P("shard"),
            P("shard", None),
            P("shard", None),
            P("shard", None),
            P("shard", None),
            P("shard"),
            P("shard", None),
            P("shard", None),
            P("shard", None),
        ),
        check_vma=False,
    )
```

profile of v0, /device:TPU:0, one launch (start us, length us, event | category | flops | bytes accessed | tf_op | source)
XLA Modules:
  0.0 299.0 jit_solution(5477235141958248480)
XLA Ops:
  0.7 2.1 slice_bitcast_fusion.1
  2.9 3.0 %collective-permute-start.4 = (bf16[384,576]{0,1:T(8,128)(2,1)}, bf16[384,576]{0,1:T(8,128)(2,1)}, u32[]{:S(2)}, u32[]{:S(2)}) collective-permute-start(bf16[384,576]{0,1:T(8,128)(2,1)} %get-tuple-element.122), channel_id=1, source_target_pairs={{0,1},{1,0},{2,3},{3,2},{4,5},{5,4},{6,7},{7,6},{8,9},{9,8},{10,11... | collective-permute-start | bytes 1327112 | tf_op jit(solution)/shard_map/ppermute | solution.py:297
  7.5 2.0 collective-permute-start
  9.5 2.1 concatenate.64
  12.7 1.9 fusion.9
  17.1 2.4 copy.112.x_ref
  20.5 2.4 copy.115.cot_ref
  22.9 13.3 %collective-permute-done = bf16[2,288]{1,0:T(2,128)(2,1)} collective-permute-done((bf16[2,288]{1,0:T(2,128)(2,1)}, bf16[2,288]{1,0:T(2,128)(2,1)}, u32[]{:S(2)}, u32[]{:S(2)}) %collective-permute-start) | collective-permute-done | bytes 1184 | tf_op jit(solution)/shard_map/ppermute | solution.py:297
  38.8 15.4 %collective-permute-done.1.far_ref = bf16[288,1536]{1,0:T(8,128)(2,1)S(1)} collective-permute-done((bf16[288,1536]{1,0:T(8,128)(2,1)}, bf16[288,1536]{1,0:T(8,128)(2,1)S(1)}, u32[]{:S(2)}, u32[]{:S(2)}) %collective-permute-start.1) | collective-permute-done | bytes 884768 | tf_op jit(solution)/shard_map/ppermute | solution.py:297
  55.1 3.6 %assemble.1 = (bf16[3,576,320]{2,1,0:T(8,128)(2,1)}, bf16[576,576]{1,0:T(8,128)(2,1)}) custom-call(s32[1]{0:T(128)} %bitcast.3.shard_ref, bf16[288,576]{1,0:T(8,128)(2,1)} %q_ref.1, bf16[288,192]{1,0:T(8,128)(2,1)} %k_ref.1, bf16[288,192]{1,0:T(8,128)(2,1)} %v_ref.1, bf16[288,576]{1,0:T(8,128)(2,1)} %o_ref.1, bf16[288,1536]{1,0:T(8,128)(2,1)} %copy-done.11), custom_call_target="tpu_custom_call" | custom-call | tf_op jit(solution)/shard_map/assemble/pallas_call | solution.py:362
  58.8 28.6 %attention_forward.1 = (bf16[3,3,1024,64]{3,2,1,0:T(8,128)(2,1)}, bf16[3,1024,64]{2,1,0:T(8,128)(2,1)}, bf16[3,1024,64]{2,1,0:T(8,128)(2,1)}, bf16[3,1024,192]{2...) custom-call(bf16[1024,576]{1,0:T(8,128)(2,1)} %copy.112.x_ref, bf16[1,576]{1,0:T(2,128)(2,1)} %slice.66.gain_ref, ...), custom_call_target="tpu_custom_call" | custom-call | flops 30000001024 | bytes 20000000 | tf_op jit(solution)/shard_map/attention_forward/pallas_call | solution.py:410
  89.0 2.3 copy.114
  91.3 1.6 select_bitcast_fusion
  92.8 2.1 maximum_select_fusion
  95.0 34.4 %mlp_both.1 = (bf16[1024,576]{1,0:T(8,128)(2,1)}, f32[1024,576]{1,0:T(8,128)}, bf16[4,2,576,384]{3,2,1,0:T(8,128)(2,1)}, bf16[4,2,448,384]{3,2,1,0:T(8,128)(2,1)}, f32[1,576]{1,0:T(1,128)}) custom-call(f32[1024,576]{1,0:T(8,128)} %get-tuple-element.32.mid_ref, bf16[1024,576]{1,0:T(8,128)(2,1)} %copy.115.cot_ref, f32[1024,1]{1,0:T(8,128)} %copy.116.live_ref, ...), custom_call_target="tpu_custom_call" | custom-call | flops 30000001024 | bytes 20000000 | tf_op jit(solution)/shard_map/mlp_both/pallas_call | solution.py:438
  129.3 2.6 dynamic-slice_bitcast_fusion
  131.9 2.4 constant_dynamic-slice_fusion.1
  136.2 16.6 %attention_backward.3 = (f32[1024,576]{1,0:T(8,128)}, bf16[4,2,80,320]{3,2,1,0:T(8,128)(2,1)}) custom-call(bf16[1024,576]{1,0:T(8,128)(2,1)} %copy.112.x_ref, bf16[1,576]{1,0:T(2,128)(2,1)} %slice.66.gain_ref, f32[1024,576]{1,0:T(8,128)} %get-tuple-element.35.gm_ref, bf16[3,3,1024,64]{3,2,1,0:T(8,128)(2,1)} %get-tuple-element.36.q_ref, ...), custom_call_target="tpu_custom_call" | custom-call | flops 15000000512 | bytes 12000000 | tf_op jit(solution)/shard_map/attention_backward/pallas_call | solution.py:491
  152.8 2.3 fusion.1.after_b_ref
  156.1 1.7 collective-permute-start.9
  157.8 1.9 fusion
  159.8 1.4 copy.123.after_a_ref
  162.1 1.5 collective-permute-start.8
  163.7 17.7 %attention_backward.4 = (f32[1024,576]{1,0:T(8,128)}, bf16[4,2,80,320]{3,2,1,0:T(8,128)(2,1)}) custom-call(bf16[1024,576]{1,0:T(8,128)(2,1)} %copy.112.x_ref, bf16[1,576]{1,0:T(2,128)(2,1)} %slice.66.gain_ref, f32[1024,576]{1,0:T(8,128)} %get-tuple-element.35.gm_ref, bf16[3,3,1024,64]{3,2,1,0:T(8,128)(2,1)} %get-tuple-element.36.q_ref, ...), custom_call_target="tpu_custom_call" | custom-call | flops 15000000512 | bytes 12000000 | tf_op jit(solution)/shard_map/attention_backward/pallas_call | solution.py:491
  184.0 2.3 fusion.2.after_a_ref
  186.3 19.1 %attention_backward.5 = (bf16[1024,576]{1,0:T(8,128)(2,1)}, bf16[4,2,80,320]{3,2,1,0:T(8,128)(2,1)}) custom-call(bf16[1024,576]{1,0:T(8,128)(2,1)} %copy.112.x_ref, bf16[1,576]{1,0:T(2,128)(2,1)} %slice.66.gain_ref, f32[1024,576]{1,0:T(8,128)} %get-tuple-element.35.gm_ref, bf16[3,3,1024,64]{3,2,1,0:T(8,128)(2,1)} %get-tuple-element.36.q_ref, ...), custom_call_target="tpu_custom_call" | custom-call | flops 15000000512 | bytes 12000000 | tf_op jit(solution)/shard_map/attention_backward/pallas_call | solution.py:491
  205.4 1.4 pad_maximum_fusion.1
  209.0 1.6 collective-permute-start.18
  210.6 2.4 copy.132
  214.3 2.4 copy.133
  216.7 2.8 collective-permute-done.18
  220.6 2.7 collective-permute-start.19
  223.5 1.6 collective-permute-start.11
  228.0 10.7 %collective-permute-done.19 = bf16[448,384]{1,0:T(8,128)(2,1)S(1)} collective-permute-done((bf16[448,384]{1,0:T(8,128)(2,1)S(1)}, bf16[448,384]{1,0:T(8,128)(2,1)S(1)}, u32[]{:S(2)}, u32[]{:S(2)}) %collective-permute-start.19) | collective-permute-done | bytes 344096 | tf_op jit(solution)/shard_map/ppermute | solution.py:297
  239.4 1.6 collective-permute-start.12
  241.0 4.1 %collective-permute-done.23 = bf16[576,384]{1,0:T(8,128)(2,1)S(1)} collective-permute-done((bf16[576,384]{1,0:T(8,128)(2,1)S(1)}, bf16[576,384]{1,0:T(8,128)(2,1)S(1)}, u32[]{:S(2)}, u32[]{:S(2)}) %collective-permute-start.23) | collective-permute-done | bytes 442400 | tf_op jit(solution)/shard_map/ppermute | solution.py:297
  245.3 1.6 collective-permute-start.24
  246.9 4.7 %collective-permute-done.12 = bf16[3,80,320]{2,1,0:T(8,128)(2,1)S(1)} collective-permute-done((bf16[3,80,320]{2,1,0:T(8,128)(2,1)S(1)}, bf16[3,80,320]{2,1,0:T(8,128)(2,1)S(1)}, u32[]{:S(2)}, u32[]{:S(2)}) %collective-permute-start.12) | collective-permute-done | bytes 153632 | tf_op jit(solution)/shard_map/ppermute | solution.py:297
  251.7 1.8 collective-permute-start.13
  253.8 5.2 %collective-permute-done.13 = bf16[3,80,320]{2,1,0:T(8,128)(2,1)S(1)} collective-permute-done((bf16[3,80,320]{2,1,0:T(8,128)(2,1)S(1)}, bf16[3,80,320]{2,1,0:T(8,128)(2,1)S(1)}, u32[]{:S(2)}, u32[]{:S(2)}) %collective-permute-start.13) | collective-permute-done | bytes 153632 | tf_op jit(solution)/shard_map/ppermute | solution.py:297
  259.0 10.1 %collective-permute-start.14 = (bf16[3,80,320]{2,1,0:T(8,128)(2,1)S(1)}, bf16[3,80,320]{2,1,0:T(8,128)(2,1)S(1)}, u32[]{:S(2)}, u32[]{:S(2)}) collective-permute-start(bf16[3,80,320]{2,1,0:T(8,128)(2,1)S(1)} %add_convert_fusion.5), channel_id=1, source_target_pairs={{0,16},{2,18},{4,20},{6,22},{8,24},{10,26},{12,28},{14,30},{16,0},... | collective-permute-start | bytes 460808 | tf_op jit(solution)/shard_map/ppermute | solution.py:297
  269.9 7.1 %collective-permute-done.14 = bf16[3,80,320]{2,1,0:T(8,128)(2,1)S(1)} collective-permute-done((bf16[3,80,320]{2,1,0:T(8,128)(2,1)S(1)}, bf16[3,80,320]{2,1,0:T(8,128)(2,1)S(1)}, u32[]{:S(2)}, u32[]{:S(2)}) %collective-permute-start.14) | collective-permute-done | bytes 153632 | tf_op jit(solution)/shard_map/ppermute | solution.py:297
  279.2 1.7 copy.137
  282.8 1.4 collective-permute-done.15
  292.5 1.4 fusion.12
  293.9 1.8 maximum_select_fusion.2
  296.0 1.4 copy.141
  297.4 1.4 copy.142
  (149 shorter events, 40.0 us)
Async XLA Ops:
  0.6 5.3 %copy-start.2 = (bf16[288,1536]{1,0:T(8,128)(2,1)S(1)}, bf16[288,1536]{1,0:T(8,128)(2,1)}, u32[]{:S(2)}) copy-start(bf16[288,1536]{1,0:T(8,128)(2,1)} %param.21) | copy-start | bytes 2654212
  0.7 5.3 %copy-start.3 = (bf16[288,1536]{1,0:T(8,128)(2,1)S(1)}, bf16[288,1536]{1,0:T(8,128)(2,1)}, u32[]{:S(2)}) copy-start(bf16[288,1536]{1,0:T(8,128)(2,1)} %param.22) | copy-start | bytes 2654212
  2.8 4.1 %copy-start.17 = (bf16[288]{0:T(512)(128)(2,1)S(1)}, bf16[288]{0:T(512)(128)(2,1)}, u32[]{:S(2)}) copy-start(bf16[288]{0:T(512)(128)(2,1)} %param.15) | copy-start | bytes 1732
  2.8 4.1 %copy-start.18 = (bf16[288]{0:T(512)(128)(2,1)S(1)}, bf16[288]{0:T(512)(128)(2,1)}, u32[]{:S(2)}) copy-start(bf16[288]{0:T(512)(128)(2,1)} %param.20) | copy-start | bytes 1732
  2.8 6.7 %copy-start.9 = (bf16[288,576]{1,0:T(8,128)(2,1)S(1)}, bf16[288,576]{1,0:T(8,128)(2,1)}, u32[]{:S(2)}) copy-start(bf16[288,576]{1,0:T(8,128)(2,1)} %q_ref.1) | copy-start | bytes 995332
  2.8 6.7 %copy-start.10 = (bf16[288,576]{1,0:T(8,128)(2,1)S(1)}, bf16[288,576]{1,0:T(8,128)(2,1)}, u32[]{:S(2)}) copy-start(bf16[288,576]{1,0:T(8,128)(2,1)} %o_ref.1) | copy-start | bytes 995332
  2.8 6.7 %copy-start.12 = (bf16[288,192]{1,0:T(8,128)(2,1)S(1)}, bf16[288,192]{1,0:T(8,128)(2,1)}, u32[]{:S(2)}) copy-start(bf16[288,192]{1,0:T(8,128)(2,1)} %k_ref.1) | copy-start | bytes 331780
  2.9 9.4 %copy-start.19 = (s32[4]{0:T(128)S(1)}, s32[4]{0:T(128)}, u32[]{:S(2)}) copy-start(s32[4]{0:T(128)} %param.13) | copy-start | bytes 52
  2.9 35.4 %collective-permute-start.4 = (bf16[384,576]{0,1:T(8,128)(2,1)}, bf16[384,576]{0,1:T(8,128)(2,1)}, u32[]{:S(2)}, u32[]{:S(2)}) collective-permute-start(bf16[384,576]{0,1:T(8,128)(2,1)} %get-tuple-element.122), channel_id=1, source_target_pairs={{0,1},{1,0},{2,3},{3,2},{4,5},{5,4},{6,7},{7,6},{8,9},{9,8},{10,11... | collective-permute-start | bytes 1327112 | tf_op jit(solution)/shard_map/ppermute | solution.py:297
  6.9 31.4 %collective-permute-start.2 = (bf16[288,1536]{1,0:T(8,128)(2,1)}, bf16[288,1536]{1,0:T(8,128)(2,1)}, u32[]{:S(2)}, u32[]{:S(2)}) collective-permute-start(bf16[288,1536]{1,0:T(8,128)(2,1)} %broadcast_select_fusion), channel_id=1, source_target_pairs={{0,1},{1,0},{2,3},{3,2},{4,5},{5,4},{6,7},{7,6},{8,9},{9,8},{10,11... | collective-permute-start | bytes 2654216 | tf_op jit(solution)/shard_map/ppermute | solution.py:297
  7.5 28.7 %collective-permute-start = (bf16[2,288]{1,0:T(2,128)(2,1)}, bf16[2,288]{1,0:T(2,128)(2,1)}, u32[]{:S(2)}, u32[]{:S(2)}) collective-permute-start(bf16[2,288]{1,0:T(2,128)(2,1)} %pad_maximum_fusion.5), channel_id=1, source_target_pairs={{0,1},{1,0},{2,3},{3,2},{4,5},{5,4},{6,7},{7,6},{8,9},{9,8},{10,11... | collective-permute-start | bytes 3464 | tf_op jit(solution)/shard_map/ppermute | solution.py:297
  11.7 42.6 %collective-permute-start.1 = (bf16[288,1536]{1,0:T(8,128)(2,1)}, bf16[288,1536]{1,0:T(8,128)(2,1)S(1)}, u32[]{:S(2)}, u32[]{:S(2)}) collective-permute-start(bf16[288,1536]{1,0:T(8,128)(2,1)} %concatenate.64), channel_id=1, source_target_pairs={{0,1},{1,0},{2,3},{3,2},{4,5},{5,4},{6,7},{7,6},{8,9},{9,8},{10,11... | collective-permute-start | bytes 2654216 | tf_op jit(solution)/shard_map/ppermute | solution.py:297
  16.0 4.5 %copy-start.15 = (s32[1024]{0:T(1024)}, s32[1024]{0:T(1024)S(1)}, u32[]{:S(2)}) copy-start(s32[1024]{0:T(1024)S(1)} %broadcast_select_fusion.3) | copy-start | bytes 12292
  19.5 16.8 %copy-start.16 = (bf16[1,2,288]{2,1,0:T(2,128)(2,1)S(1)}, bf16[1,2,288]{2,1,0:T(2,128)(2,1)}, u32[]{:S(2)}) copy-start(bf16[1,2,288]{2,1,0:T(2,128)(2,1)} %fusion.19) | copy-start | bytes 3460
  38.3 49.1 %collective-permute-start.5 = (bf16[384,576]{0,1:T(8,128)(2,1)}, bf16[384,576]{0,1:T(8,128)(2,1)S(1)}, u32[]{:S(2)}, u32[]{:S(2)}) collective-permute-start(bf16[384,576]{0,1:T(8,128)(2,1)} %collective-permute-done.4), channel_id=1, source_target_pairs={{0,2},{2,0},{4,6},{6,4},{8,10},{10,8},{12,14},{14,12},{16,18},{18,... | collective-permute-start | bytes 1327112 | tf_op jit(solution)/shard_map/ppermute | solution.py:297
  38.3 53.0 %collective-permute-start.3 = (bf16[288,1536]{1,0:T(8,128)(2,1)}, bf16[288,1536]{1,0:T(8,128)(2,1)}, u32[]{:S(2)}, u32[]{:S(2)}) collective-permute-start(bf16[288,1536]{1,0:T(8,128)(2,1)} %collective-permute-done.2), channel_id=1, source_target_pairs={{0,2},{2,0},{4,6},{6,4},{8,10},{10,8},{12,14},{14,12},{16,18},{18,... | collective-permute-start | bytes 2654216 | tf_op jit(solution)/shard_map/ppermute | solution.py:297
  54.2 0.9 copy-start.11
  131.9 20.9 %collective-permute-start.7 = (bf16[2,2,448,384]{3,2,1,0:T(8,128)(2,1)}, bf16[2,2,448,384]{3,2,1,0:T(8,128)(2,1)}, u32[]{:S(2)}, u32[]{:S(2)}) collective-permute-start(bf16[2,2,448,384]{3,2,1,0:T(8,128)(2,1)} %dynamic-slice_bitcast_fusion), channel_id=1, source_target_pairs={{0,2},{2,0},{4,6},{6,4},{8,10},{10,8},{12,14},{14,12},{16,18},{18,... | collective-permute-start | bytes 4128776 | tf_op jit(solution)/shard_map/ppermute | solution.py:297
  134.5 23.4 %collective-permute-start.6 = (bf16[2,2,576,384]{3,2,0,1:T(8,128)(2,1)S(1)}, bf16[2,2,576,384]{3,2,0,1:T(8,128)(2,1)}, u32[]{:S(2)}, u32[]{:S(2)}) collective-permute-start(bf16[2,2,576,384]{3,2,0,1:T(8,128)(2,1)S(1)} %bitcast.148), channel_id=1, source_target_pairs={{0,2},{2,0},{4,6},{6,4},{8,10},{10,8},{12,14},{14,12},{16,18},{18,... | collective-permute-start | bytes 5308424 | tf_op jit(solution)/shard_map/ppermute | solution.py:297
  155.1 2.8 copy-start
  156.1 25.2 %collective-permute-start.9 = (bf16[2,448,384]{2,1,0:T(8,128)(2,1)}, bf16[2,448,384]{2,1,0:T(8,128)(2,1)}, u32[]{:S(2)}, u32[]{:S(2)}) collective-permute-start(bf16[2,448,384]{2,1,0:T(8,128)(2,1)} %dynamic-slice_bitcast_fusion.3), channel_id=1, source_target_pairs={{0,4},{2,6},{4,0},{6,2},{8,12},{10,14},{12,8},{14,10},{16,20},{18,... | collective-permute-start | bytes 2064392 | tf_op jit(solution)/shard_map/ppermute | solution.py:297
  162.1 21.9 %collective-permute-start.8 = (bf16[2,576,384]{2,1,0:T(8,128)(2,1)}, bf16[2,576,384]{2,1,0:T(8,128)(2,1)}, u32[]{:S(2)}, u32[]{:S(2)}) collective-permute-start(bf16[2,576,384]{2,1,0:T(8,128)(2,1)} %dynamic-slice_bitcast_fusion.1), channel_id=1, source_target_pairs={{0,1},{1,0},{2,3},{3,2},{4,5},{5,4},{6,7},{7,6},{8,9},{9,8},{10,11... | collective-permute-start | bytes 2654216 | tf_op jit(solution)/shard_map/ppermute | solution.py:297
  163.7 17.7 %copy-start.1 = (bf16[2,2,448,384]{3,2,1,0:T(8,128)(2,1)S(1)}, bf16[2,2,448,384]{3,2,1,0:T(8,128)(2,1)}, u32[]{:S(2)}) copy-start(bf16[2,2,448,384]{3,2,1,0:T(8,128)(2,1)} %copy-done) | copy-start | bytes 4128772
  182.6 3.6 %copy-start.5 = (bf16[2,448,384]{2,1,0:T(8,128)(2,1)}, bf16[2,448,384]{2,1,0:T(8,128)(2,1)S(1)}, u32[]{:S(2)}) copy-start(bf16[2,448,384]{2,1,0:T(8,128)(2,1)S(1)} %fusion.4.after_b_ref) | copy-start | bytes 2064388
  183.5 24.3 %collective-permute-start.17 = (bf16[448,384]{1,0:T(8,128)(2,1)}, bf16[448,384]{1,0:T(8,128)(2,1)}, u32[]{:S(2)}, u32[]{:S(2)}) collective-permute-start(bf16[448,384]{1,0:T(8,128)(2,1)} %dynamic-slice_bitcast_fusion.6), channel_id=1, source_target_pairs={{0,1},{1,0},{2,3},{3,2},{4,5},{5,4},{6,7},{7,6},{8,9},{9,8},{10,11... | collective-permute-start | bytes 1032200 | tf_op jit(solution)/shard_map/ppermute | solution.py:297
  186.3 19.1 %copy-start.13 = (bf16[4,2,80,320]{3,2,1,0:T(8,128)(2,1)S(1)}, bf16[4,2,80,320]{3,2,1,0:T(8,128)(2,1)}, u32[]{:S(2)}) copy-start(bf16[4,2,80,320]{3,2,1,0:T(8,128)(2,1)} %get-tuple-element.46) | copy-start | bytes 1228804
  186.3 19.1 %copy-start.14 = (bf16[4,2,80,320]{3,2,1,0:T(8,128)(2,1)S(1)}, bf16[4,2,80,320]{3,2,1,0:T(8,128)(2,1)}, u32[]{:S(2)}) copy-start(bf16[4,2,80,320]{3,2,1,0:T(8,128)(2,1)} %get-tuple-element.47) | copy-start | bytes 1228804
  205.4 2.4 copy-start.6
  207.8 5.2 %copy-start.4 = (bf16[2,576,384]{2,1,0:T(8,128)(2,1)S(1)}, bf16[2,576,384]{2,1,0:T(8,128)(2,1)}, u32[]{:S(2)}) copy-start(bf16[2,576,384]{2,1,0:T(8,128)(2,1)} %fusion.2.after_a_ref) | copy-start | bytes 2654212
  207.8 15.5 %collective-permute-start.10 = (bf16[2,2,3,80,320]{4,3,1,0,2:T(8,128)(2,1)}, bf16[2,2,3,80,320]{4,3,1,0,2:T(8,128)(2,1)S(1)}, u32[]{:S(2)}, u32[]{:S(2)}) collective-permute-start(bf16[2,2,3,80,320]{4,3,1,0,2:T(8,128)(2,1)} %dynamic-slice_bitcast_fusion.2), channel_id=1, source_target_pairs={{0,2},{2,0},{4,6},{6,4},{8,10},{10,8},{12,14},{14,12},{16,18},{18,... | collective-permute-start | bytes 1843208 | tf_op jit(solution)/shard_map/ppermute | solution.py:297
  209.0 10.6 %collective-permute-start.18 = (bf16[448,384]{1,0:T(8,128)(2,1)S(1)}, bf16[448,384]{1,0:T(8,128)(2,1)}, u32[]{:S(2)}, u32[]{:S(2)}) collective-permute-start(bf16[448,384]{1,0:T(8,128)(2,1)S(1)} %fusion.7), channel_id=1, source_target_pairs={{0,8},{2,10},{4,12},{6,14},{8,0},{10,2},{12,4},{14,6},{16,24},{18,... | collective-permute-start | bytes 1032200 | tf_op jit(solution)/shard_map/ppermute | solution.py:297
  213.8 12.5 %collective-permute-start.22 = (bf16[576,384]{1,0:T(8,128)(2,1)}, bf16[576,384]{1,0:T(8,128)(2,1)}, u32[]{:S(2)}, u32[]{:S(2)}) collective-permute-start(bf16[576,384]{1,0:T(8,128)(2,1)} %dynamic-slice_bitcast_fusion.4), channel_id=1, source_target_pairs={{0,4},{2,6},{4,0},{6,2},{8,12},{10,14},{12,8},{14,10},{16,20},{18,... | collective-permute-start | bytes 1327112 | tf_op jit(solution)/shard_map/ppermute | solution.py:297
  220.6 18.0 %collective-permute-start.19 = (bf16[448,384]{1,0:T(8,128)(2,1)S(1)}, bf16[448,384]{1,0:T(8,128)(2,1)S(1)}, u32[]{:S(2)}, u32[]{:S(2)}) collective-permute-start(bf16[448,384]{1,0:T(8,128)(2,1)S(1)} %add_convert_fusion.3), channel_id=1, source_target_pairs={{0,16},{2,18},{4,20},{6,22},{8,24},{10,26},{12,28},{14,30},{16,0},... | collective-permute-start | bytes 1032200 | tf_op jit(solution)/shard_map/ppermute | solution.py:297
  223.5 15.8 %collective-permute-start.11 = (bf16[2,3,80,320]{3,2,0,1:T(8,128)(2,1)S(1)}, bf16[2,3,80,320]{3,2,0,1:T(8,128)(2,1)S(1)}, u32[]{:S(2)}, u32[]{:S(2)}) collective-permute-start(bf16[2,3,80,320]{3,2,0,1:T(8,128)(2,1)S(1)} %dynamic-slice_bitcast_fusion.5), channel_id=1, source_target_pairs={{0,1},{1,0},{2,3},{3,2},{4,5},{5,4},{6,7},{7,6},{8,9},{9,8},{10,11... | collective-permute-start | bytes 921608 | tf_op jit(solution)/shard_map/ppermute | solution.py:297
  227.5 17.7 %collective-permute-start.23 = (bf16[576,384]{1,0:T(8,128)(2,1)S(1)}, bf16[576,384]{1,0:T(8,128)(2,1)S(1)}, u32[]{:S(2)}, u32[]{:S(2)}) collective-permute-start(bf16[576,384]{1,0:T(8,128)(2,1)S(1)} %fusion.5), channel_id=1, source_target_pairs={{0,8},{2,10},{4,12},{6,14},{8,0},{10,2},{12,4},{14,6},{16,24},{18,... | collective-permute-start | bytes 1327112 | tf_op jit(solution)/shard_map/ppermute | solution.py:297
  238.7 14.7 %collective-permute-start.20 = (bf16[448,384]{1,0:T(8,128)(2,1)S(1)}, bf16[448,384]{1,0:T(8,128)(2,1)S(1)}, u32[]{:S(2)}, u32[]{:S(2)}) collective-permute-start(bf16[448,384]{1,0:T(8,128)(2,1)S(1)} %add_convert_fusion.2), channel_id=1, source_target_pairs={{0,4},{2,6},{4,0},{6,2},{8,12},{10,14},{12,8},{14,10},{16,20},{18,... | collective-permute-start | bytes 1032200 | tf_op jit(solution)/shard_map/ppermute | solution.py:297
  239.4 12.2 %collective-permute-start.12 = (bf16[3,80,320]{2,1,0:T(8,128)(2,1)S(1)}, bf16[3,80,320]{2,1,0:T(8,128)(2,1)S(1)}, u32[]{:S(2)}, u32[]{:S(2)}) collective-permute-start(bf16[3,80,320]{2,1,0:T(8,128)(2,1)S(1)} %dynamic-slice_bitcast_fusion.7), channel_id=1, source_target_pairs={{0,4},{2,6},{4,0},{6,2},{8,12},{10,14},{12,8},{14,10},{16,20},{18,... | collective-permute-start | bytes 460808 | tf_op jit(solution)/shard_map/ppermute | solution.py:297
  245.3 23.8 %collective-permute-start.24 = (bf16[576,384]{1,0:T(8,128)(2,1)S(1)}, bf16[576,384]{1,0:T(8,128)(2,1)S(1)}, u32[]{:S(2)}, u32[]{:S(2)}) collective-permute-start(bf16[576,384]{1,0:T(8,128)(2,1)S(1)} %add_convert_fusion.1), channel_id=1, source_target_pairs={{0,16},{2,18},{4,20},{6,22},{8,24},{10,26},{12,28},{14,30},{16,0},... | collective-permute-start | bytes 1327112 | tf_op jit(solution)/shard_map/ppermute | solution.py:297
  251.7 7.3 %collective-permute-start.13 = (bf16[3,80,320]{2,1,0:T(8,128)(2,1)S(1)}, bf16[3,80,320]{2,1,0:T(8,128)(2,1)S(1)}, u32[]{:S(2)}, u32[]{:S(2)}) collective-permute-start(bf16[3,80,320]{2,1,0:T(8,128)(2,1)S(1)} %fusion.8), channel_id=1, source_target_pairs={{0,8},{2,10},{4,12},{6,14},{8,0},{10,2},{12,4},{14,6},{16,24},{18,... | collective-permute-start | bytes 460808 | tf_op jit(solution)/shard_map/ppermute | solution.py:297
  253.6 24.0 %collective-permute-start.21 = (bf16[2,448,384]{2,1,0:T(8,128)(2,1)S(1)}, bf16[2,448,384]{2,1,0:T(8,128)(2,1)S(1)}, u32[]{:S(2)}, u32[]{:S(2)}) collective-permute-start(bf16[2,448,384]{2,1,0:T(8,128)(2,1)S(1)} %maximum_select_fusion.10), channel_id=1, source_target_pairs={{0,2},{2,0},{4,6},{6,4},{8,10},{10,8},{12,14},{14,12},{16,18},{18,... | collective-permute-start | bytes 2064392 | tf_op jit(solution)/shard_map/ppermute | solution.py:297
  259.0 18.0 %collective-permute-start.14 = (bf16[3,80,320]{2,1,0:T(8,128)(2,1)S(1)}, bf16[3,80,320]{2,1,0:T(8,128)(2,1)S(1)}, u32[]{:S(2)}, u32[]{:S(2)}) collective-permute-start(bf16[3,80,320]{2,1,0:T(8,128)(2,1)S(1)} %add_convert_fusion.5), channel_id=1, source_target_pairs={{0,16},{2,18},{4,20},{6,22},{8,24},{10,26},{12,28},{14,30},{16,0},... | collective-permute-start | bytes 460808 | tf_op jit(solution)/shard_map/ppermute | solution.py:297
  269.3 15.2 %collective-permute-start.25 = (bf16[576,384]{1,0:T(8,128)(2,1)S(1)}, bf16[576,384]{1,0:T(8,128)(2,1)S(1)}, u32[]{:S(2)}, u32[]{:S(2)}) collective-permute-start(bf16[576,384]{1,0:T(8,128)(2,1)S(1)} %add_convert_fusion), channel_id=1, source_target_pairs={{0,4},{2,6},{4,0},{6,2},{8,12},{10,14},{12,8},{14,10},{16,20},{18,... | collective-permute-start | bytes 1327112 | tf_op jit(solution)/shard_map/ppermute | solution.py:297
  277.1 7.1 %collective-permute-start.15 = (bf16[3,80,320]{2,1,0:T(8,128)(2,1)S(1)}, bf16[3,80,320]{2,1,0:T(8,128)(2,1)S(1)}, u32[]{:S(2)}, u32[]{:S(2)}) collective-permute-start(bf16[3,80,320]{2,1,0:T(8,128)(2,1)S(1)} %add_convert_fusion.4), channel_id=1, source_target_pairs={{0,4},{2,6},{4,0},{6,2},{8,12},{10,14},{12,8},{14,10},{16,20},{18,... | collective-permute-start | bytes 460808 | tf_op jit(solution)/shard_map/ppermute | solution.py:297
  284.3 3.1 %collective-permute-start.16 = (bf16[2,3,80,320]{3,2,1,0:T(8,128)(2,1)S(1)}, bf16[2,3,80,320]{3,2,1,0:T(8,128)(2,1)S(1)}, u32[]{:S(2)}, u32[]{:S(2)}) collective-permute-start(bf16[2,3,80,320]{3,2,1,0:T(8,128)(2,1)S(1)} %maximum_select_fusion.12), channel_id=1, source_target_pairs={{0,2},{2,0},{4,6},{6,4},{8,10},{10,8},{12,14},{14,12},{16,18},{18,... | collective-permute-start | bytes 921608 | tf_op jit(solution)/shard_map/ppermute | solution.py:297
  284.5 1.6 copy-start.8
  285.6 8.3 %collective-permute-start.26 = (bf16[2,576,384]{2,1,0:T(8,128)(2,1)}, bf16[2,576,384]{2,1,0:T(8,128)(2,1)}, u32[]{:S(2)}, u32[]{:S(2)}) collective-permute-start(bf16[2,576,384]{2,1,0:T(8,128)(2,1)} %maximum_select_fusion.7), channel_id=1, source_target_pairs={{0,2},{2,0},{4,6},{6,4},{8,10},{10,8},{12,14},{14,12},{16,18},{18,... | collective-permute-start | bytes 2654216 | tf_op jit(solution)/shard_map/ppermute | solution.py:297
  287.8 0.9 copy-start.7
where the time goes:
time: 304 us; the launch traced here: 299 us
  Pallas kernels  120 us (39%)
  waiting for transfers between devices  66 us (22%)
  local copies, waits for them, and re-layouts  40.9 us (13%)
  other arithmetic  36.4 us (12%)
  starting transfers between devices  34.4 us (11%)
    ppermute x27, waiting for transfers between devices, swap(): return lax.ppermute(array, axis, [(i, i ^ bit) for i in range(size)])  66 us
    pallas_call x3, Pallas kernels, local(): pl.pallas_call(functools.partial(backward_kernel, first, last), grid=(1,)...  53.4 us
    ppermute x27, starting transfers between devices, swap(): return lax.ppermute(array, axis, [(i, i ^ bit) for i in range(size)])  34.4 us
    pallas_call x1, Pallas kernels, local(): pl.pallas_call(mlp_kernel, grid=(steps,), in_specs=[row_block, row_block,...  34.4 us
    pallas_call x1, Pallas kernels, local(): pl.pallas_call(forward_kernel, grid=(KV_HEADS,), in_specs=[row_block, gai...  28.6 us
    unnamed x50, local copies, waits for them, and re-layouts  16.3 us
    convert_element_type x9, other arithmetic, halve(): return (take(array, mine).astype(F32) + sent.astype(F32)).astype(BF16)  10.4 us
    select_n x11, other arithmetic, both(): jnp.where(mine == 0, jnp.stack([array, other]), jnp.stack([other, array]))  7.64 us
  transfers between devices with their start and end apart: 27, of which 10 were waited for; matrix products, arithmetic and copies ran while one was open for 21% of the time, Pallas kernels for 29%

commit v1 on v0

--- a/solution.py
+++ b/solution.py
@@ -72,10 +72,11 @@
 
 
 def forward_kernel(
-    x_ref, gain_ref, wqkv_ref, wout_ref, cos_ref, sin_ref, lcol_ref, lrow_ref,
-    q_ref, k_ref, v_ref, att_ref, lse_ref, mid_ref, n1_ref,
+    x_ref, gain_ref, wqkv_ref, wout_ref, cos_ref, sin_ref, lcol_ref, lrow_ref, core_ref,
+    q_ref, k_ref, v_ref, att_ref, lse_ref, mid_ref, core_out_ref, n1_ref,
 ):
     rows = x_ref.shape[0]
+    core_out_ref[0] = core_ref[0]
 
     @pl.when(pl.program_id(0) == 0)
     def _():
@@ -250,9 +251,10 @@
         xg_ref[...] = gn_ref[...]
 
 
-def assemble_kernel(shard_ref, q_ref, k_ref, v_ref, o_ref, far_ref, qkv_ref, out_ref):
+def assemble_kernel(shard_ref, q_ref, k_ref, v_ref, o_ref, far_ref, qkv_ref, out_ref, core_ref):
     rows = q_ref.shape[0]
     shard = shard_ref[0]
+    core_ref[0] = shard_ref[1]
     starts = (0, q_ref.shape[1], q_ref.shape[1] + k_ref.shape[1])
     starts = starts + (starts[2] + v_ref.shape[1],)
 
@@ -327,8 +329,12 @@
     yield array.reshape((4,) + array.shape[2:])
 
 
-def gather_halves(first, second, core, shard, n_rep):
-    got = swap(jnp.where(core == 0, first, second), "shard", 2, 1)
+def fetch_half(first, second, core):
+    return swap(jnp.where(core == 0, first, second), "shard", 2, 1)
+
+
+def exchange_halves(first, second, got, core, shard, n_rep):
+    got = jnp.where(core < 2, got, jnp.zeros_like(got))
     other = swap(got, "rep", n_rep, 1)
     far_first = jnp.where(core == 0, got, other)
     far_second = jnp.where(core == 0, other, got)
@@ -359,25 +365,26 @@
         far_gains = swap(gains, "shard", 2, 1)
         gains = both(gains, far_gains, shard).swapaxes(0, 1).reshape(2, width)
         gain_one, gain_two = gains[:1], gains[1:]
-        qkv_full, out_full = pl.pallas_call(
+        qkv_full, out_full, late_core = pl.pallas_call(
             assemble_kernel,
             in_specs=[pl.BlockSpec(memory_space=pltpu.SMEM)]
             + [pl.BlockSpec(memory_space=pltpu.VMEM)] * 5,
-            out_specs=[pl.BlockSpec(memory_space=pltpu.VMEM)] * 2,
+            out_specs=[pl.BlockSpec(memory_space=pltpu.VMEM)] * 2
+            + [pl.BlockSpec(memory_space=pltpu.SMEM)],
             out_shape=[
                 jax.ShapeDtypeStruct((KV_HEADS, width, packed_width), BF16),
                 jax.ShapeDtypeStruct((width, width), BF16),
+                jax.ShapeDtypeStruct((1,), jnp.int32),
             ],
             compiler_params=params(),
             name="assemble",
-        )(shard[None], w_query, w_key, w_value, w_out, far)
-        gate_full, up_full = gather_halves(w_gate, w_up, core, shard, n_rep)
+        )(jnp.stack([shard, core]).astype(jnp.int32), w_query, w_key, w_value, w_out, far)
+        late = late_core[0]
         down_half = w_down.shape[0] // 2
-        top, low = gather_halves(w_down[:down_half], w_down[down_half:], core, shard, n_rep)
-        down_full = jnp.concatenate(
-            [top.reshape(2, down_half, width), low.reshape(2, down_half, width)], axis=1
-        ).reshape(-1, width)
+        got_wide = fetch_half(w_gate, w_up, late)
+        got_down = fetch_half(w_down[:down_half], w_down[down_half:], late)
     else:
+        late_core = core.astype(jnp.int32)[None]
         gather = functools.partial(lax.all_gather, axis_name="shard", axis=0, tiled=True)
         qkv = jnp.concatenate(
             [
@@ -407,12 +414,14 @@
     out_block = lead((group_width, width))
     tables = [whole((rows, HEAD_DIM))] * 2 + [whole((rows, 1)), whole((1, rows))]
     row_block, gain_block = whole((rows, width)), whole((1, width))
-    queries, keys, values, attended, lse, middle = pl.pallas_call(
+    queries, keys, values, attended, lse, middle, later_core = pl.pallas_call(
         forward_kernel,
         grid=(KV_HEADS,),
-        in_specs=[row_block, gain_block, qkv_block, out_block] + tables,
+        in_specs=[row_block, gain_block, qkv_block, out_block] + tables
+        + [pl.BlockSpec(memory_space=pltpu.SMEM)],
         out_specs=[
             head_block, kv_block, kv_block, lead((1, rows, group_width)), lse_block, row_block,
+            pl.BlockSpec(memory_space=pltpu.SMEM),
         ],
         out_shape=[
             shape((KV_HEADS, GROUP, rows, HEAD_DIM), BF16),
@@ -421,6 +430,7 @@
             shape((KV_HEADS, rows, group_width), BF16),
             shape((KV_HEADS, rows, GROUP), F32),
             shape((rows, width), F32),
+            shape((1,), jnp.int32),
         ],
         scratch_shapes=[pltpu.VMEM((rows, width), BF16)],
         compiler_params=params(),
@@ -428,7 +438,17 @@
             flops=30_000_000_000, bytes_accessed=20_000_000, transcendentals=6_000_000
         ),
         name="attention_forward",
-    )(layer_input, gain_one, qkv_full, out_full, cos_full, sin_full, label_col, label_row)
+    )(layer_input, gain_one, qkv_full, out_full, cos_full, sin_full, label_col, label_row, late_core)
+
+    if quick:
+        later = later_core[0]
+        gate_full, up_full = exchange_halves(w_gate, w_up, got_wide, later, shard, n_rep)
+        top, low = exchange_halves(
+            w_down[:down_half], w_down[down_half:], got_down, later, shard, n_rep
+        )
+        down_full = jnp.concatenate(
+            [top.reshape(2, down_half, width), low.reshape(2, down_half, width)], axis=1
+        ).reshape(-1, width)
 
     steps, parts = 2, 4
     chunk, per_step = ff // steps, parts // steps

time: 304 us -> 290 us (0.954)
  waiting for transfers between devices: 66 us -> 49.6 us
    ppermute x27, waiting for transfers between devices: 66 us -> 49.6 us  [swap(): return lax.ppermute(array, axis, [(i, i ^ bit) for i in range(size)])]
  transfers between devices with their start and end apart: 27 -> 27, of which waited for: 10 -> 9; matrix products, arithmetic and copies ran while one was open for 21% -> 21% of each run, Pallas kernels for 29% -> 29%
where the time goes in v1:
time: 290 us; the launch traced here: 285 us
  Pallas kernels  121 us (42%)
  waiting for transfers between devices  49.6 us (17%)
  local copies, waits for them, and re-layouts  40.9 us (14%)
  other arithmetic  36.5 us (13%)
  starting transfers between devices  34.4 us (12%)
  between operations  3.2 us (1%)
    pallas_call x3, Pallas kernels, local(): pl.pallas_call(functools.partial(backward_kernel, first, last), grid=(1,)...  53.3 us
    ppermute x27, waiting for transfers between devices, swap(): return lax.ppermute(array, axis, [(i, i ^ bit) for i in range(size)])  49.6 us
    ppermute x27, starting transfers between devices, swap(): return lax.ppermute(array, axis, [(i, i ^ bit) for i in range(size)])  34.4 us
    pallas_call x1, Pallas kernels, local(): pl.pallas_call(mlp_kernel, grid=(steps,), in_specs=[row_block, row_block,...  34.4 us
    pallas_call x1, Pallas kernels, local(): pl.pallas_call(forward_kernel, grid=(KV_HEADS,), in_specs=[row_block, gai...  29.5 us
    unnamed x50, local copies, waits for them, and re-layouts  16.1 us
    convert_element_type x9, other arithmetic, halve(): return (take(array, mine).astype(F32) + sent.astype(F32)).astype(BF16)  10.4 us
    select_n x11, other arithmetic, both(): jnp.where(mine == 0, jnp.stack([array, other]), jnp.stack([other, array]))  7.69 us
  transfers between devices with their start and end apart: 27, of which 9 were waited for; matrix products, arithmetic and copies ran while one was open for 21% of the time, Pallas kernels for 29%

profile of v1, /device:TPU:0, one launch (start us, length us, event | category | flops | bytes accessed | tf_op | source)
XLA Modules:
  0.0 285.4 jit_solution(17854271048818349886)
XLA Ops:
  0.7 2.3 concatenate.64
  3.0 3.0 %collective-permute-start.1 = (bf16[288,1536]{1,0:T(8,128)(2,1)}, bf16[288,1536]{1,0:T(8,128)(2,1)S(1)}, u32[]{:S(2)}, u32[]{:S(2)}) collective-permute-start(bf16[288,1536]{1,0:T(8,128)(2,1)} %concatenate.64), channel_id=1, source_target_pairs={{0,1},{1,0},{2,3},{3,2},{4,5},{5,4},{6,7},{7,6},{8,9},{9,8},{10,11... | collective-permute-start | bytes 2654216 | tf_op jit(solution)/shard_map/ppermute | solution.py:299
  6.5 1.9 fusion.9
  12.2 1.4 copy.112.x_ref
  13.6 12.2 %collective-permute-done = bf16[2,288]{1,0:T(2,128)(2,1)S(1)} collective-permute-done((bf16[2,288]{1,0:T(2,128)(2,1)S(1)}, bf16[2,288]{1,0:T(2,128)(2,1)S(1)}, u32[]{:S(2)}, u32[]{:S(2)}) %collective-permute-start) | collective-permute-done | bytes 1184 | tf_op jit(solution)/shard_map/ppermute | solution.py:299
  27.5 3.6 %assemble.1 = (bf16[3,576,320]{2,1,0:T(8,128)(2,1)}, bf16[576,576]{1,0:T(8,128)(2,1)}, s32[1]{0:T(128)}) custom-call(s32[2]{0:T(128)} %pad_add_fusion.shard_ref, bf16[288,576]{1,0:T(8,128)(2,1)} %q_ref.1, bf16[288,192]{1,0:T(8,128)(2,1)} %k_ref.1, bf16[288,192]{1,0:T(8,128)(2,1)} %v_ref.1, bf16[288,576]{1,0:T(8,128)(2,1)} %o_ref.1, bf16[288,1536]{1,0:T(8,128)(2,1)} %copy-done.13), custom_call_target="tpu_custom_call" | custom-call | tf_op jit(solution)/shard_map/assemble/pallas_call | solution.py:368
  32.7 1.7 collective-permute-start.4
  35.8 29.5 %attention_forward.1 = (bf16[3,3,1024,64]{3,2,1,0:T(8,128)(2,1)}, bf16[3,1024,64]{2,1,0:T(8,128)(2,1)}, bf16[3,1024,64]{2,1,0:T(8,128)(2,1)}, bf16[3,1024,192]{2...) custom-call(bf16[1024,576]{1,0:T(8,128)(2,1)} %copy.112.x_ref, ...), custom_call_target="tpu_custom_call" | custom-call | flops 30000001024 | bytes 20000000 | tf_op jit(solution)/shard_map/attention_forward/pallas_call | solution.py:417
  69.3 2.4 copy.115.cot_ref
  74.6 2.3 copy.114
  76.9 1.6 select_bitcast_fusion
  78.4 2.1 maximum_select_fusion
  80.5 34.4 %mlp_both.1 = (bf16[1024,576]{1,0:T(8,128)(2,1)}, f32[1024,576]{1,0:T(8,128)}, bf16[4,2,576,384]{3,2,1,0:T(8,128)(2,1)}, bf16[4,2,448,384]{3,2,1,0:T(8,128)(2,1)}, f32[1,576]{1,0:T(1,128)}) custom-call(f32[1024,576]{1,0:T(8,128)} %get-tuple-element.35.mid_ref, bf16[1024,576]{1,0:T(8,128)(2,1)} %copy.115.cot_ref, f32[1024,1]{1,0:T(8,128)} %copy.116.live_ref, ...), custom_call_target="tpu_custom_call" | custom-call | flops 30000001024 | bytes 20000000 | tf_op jit(solution)/shard_map/mlp_both/pallas_call | solution.py:458
  114.9 2.6 dynamic-slice_bitcast_fusion
  117.5 2.4 constant_dynamic-slice_fusion.1
  121.8 16.6 %attention_backward.3 = (f32[1024,576]{1,0:T(8,128)}, bf16[4,2,80,320]{3,2,1,0:T(8,128)(2,1)}) custom-call(bf16[1024,576]{1,0:T(8,128)(2,1)} %copy.112.x_ref, bf16[1,576]{1,0:T(2,128)(2,1)} %slice.68.gain_ref, f32[1024,576]{1,0:T(8,128)} %get-tuple-element.39.gm_ref, bf16[3,3,1024,64]{3,2,1,0:T(8,128)(2,1)} %get-tuple-element.40.q_ref, ...), custom_call_target="tpu_custom_call" | custom-call | flops 15000000512 | bytes 12000000 | tf_op jit(solution)/shard_map/attention_backward/pallas_call | solution.py:511
  138.4 2.3 fusion.1.after_b_ref
  141.7 1.7 collective-permute-start.9
  143.5 1.9 fusion
  145.4 1.4 copy.123.after_a_ref
  147.7 1.5 collective-permute-start.8
  149.3 17.7 %attention_backward.4 = (f32[1024,576]{1,0:T(8,128)}, bf16[4,2,80,320]{3,2,1,0:T(8,128)(2,1)}) custom-call(bf16[1024,576]{1,0:T(8,128)(2,1)} %copy.112.x_ref, bf16[1,576]{1,0:T(2,128)(2,1)} %slice.68.gain_ref, f32[1024,576]{1,0:T(8,128)} %get-tuple-element.39.gm_ref, bf16[3,3,1024,64]{3,2,1,0:T(8,128)(2,1)} %get-tuple-element.40.q_ref, ...), custom_call_target="tpu_custom_call" | custom-call | flops 15000000512 | bytes 12000000 | tf_op jit(solution)/shard_map/attention_backward/pallas_call | solution.py:511
  166.9 1.3 fusion.4.after_b_ref
  170.4 2.3 fusion.2.after_a_ref
  172.7 19.1 %attention_backward.5 = (bf16[1024,576]{1,0:T(8,128)(2,1)}, bf16[4,2,80,320]{3,2,1,0:T(8,128)(2,1)}) custom-call(bf16[1024,576]{1,0:T(8,128)(2,1)} %copy.112.x_ref, bf16[1,576]{1,0:T(2,128)(2,1)} %slice.68.gain_ref, f32[1024,576]{1,0:T(8,128)} %get-tuple-element.39.gm_ref, bf16[3,3,1024,64]{3,2,1,0:T(8,128)(2,1)} %get-tuple-element.40.q_ref, ...), custom_call_target="tpu_custom_call" | custom-call | flops 15000000512 | bytes 12000000 | tf_op jit(solution)/shard_map/attention_backward/pallas_call | solution.py:511
  191.8 1.4 pad_maximum_fusion.1
  195.3 1.6 collective-permute-start.18
  197.0 2.4 copy.132
  200.7 2.4 copy.133
  203.1 2.8 collective-permute-done.18
  207.0 2.7 collective-permute-start.19
  209.9 1.6 collective-permute-start.11
  214.3 10.7 %collective-permute-done.19 = bf16[448,384]{1,0:T(8,128)(2,1)S(1)} collective-permute-done((bf16[448,384]{1,0:T(8,128)(2,1)S(1)}, bf16[448,384]{1,0:T(8,128)(2,1)S(1)}, u32[]{:S(2)}, u32[]{:S(2)}) %collective-permute-start.19) | collective-permute-done | bytes 344096 | tf_op jit(solution)/shard_map/ppermute | solution.py:299
  225.8 1.6 collective-permute-start.12
  227.4 4.1 %collective-permute-done.23 = bf16[576,384]{1,0:T(8,128)(2,1)S(1)} collective-permute-done((bf16[576,384]{1,0:T(8,128)(2,1)S(1)}, bf16[576,384]{1,0:T(8,128)(2,1)S(1)}, u32[]{:S(2)}, u32[]{:S(2)}) %collective-permute-start.23) | collective-permute-done | bytes 442400 | tf_op jit(solution)/shard_map/ppermute | solution.py:299
  231.7 1.6 collective-permute-start.24
  233.3 4.7 %collective-permute-done.12 = bf16[3,80,320]{2,1,0:T(8,128)(2,1)S(1)} collective-permute-done((bf16[3,80,320]{2,1,0:T(8,128)(2,1)S(1)}, bf16[3,80,320]{2,1,0:T(8,128)(2,1)S(1)}, u32[]{:S(2)}, u32[]{:S(2)}) %collective-permute-start.12) | collective-permute-done | bytes 153632 | tf_op jit(solution)/shard_map/ppermute | solution.py:299
  238.0 1.8 collective-permute-start.13
  240.2 5.2 %collective-permute-done.13 = bf16[3,80,320]{2,1,0:T(8,128)(2,1)S(1)} collective-permute-done((bf16[3,80,320]{2,1,0:T(8,128)(2,1)S(1)}, bf16[3,80,320]{2,1,0:T(8,128)(2,1)S(1)}, u32[]{:S(2)}, u32[]{:S(2)}) %collective-permute-start.13) | collective-permute-done | bytes 153632 | tf_op jit(solution)/shard_map/ppermute | solution.py:299
  245.4 10.1 %collective-permute-start.14 = (bf16[3,80,320]{2,1,0:T(8,128)(2,1)S(1)}, bf16[3,80,320]{2,1,0:T(8,128)(2,1)S(1)}, u32[]{:S(2)}, u32[]{:S(2)}) collective-permute-start(bf16[3,80,320]{2,1,0:T(8,128)(2,1)S(1)} %add_convert_fusion.5), channel_id=1, source_target_pairs={{0,16},{2,18},{4,20},{6,22},{8,24},{10,26},{12,28},{14,30},{16,0},... | collective-permute-start | bytes 460808 | tf_op jit(solution)/shard_map/ppermute | solution.py:299
  256.2 7.1 %collective-permute-done.14 = bf16[3,80,320]{2,1,0:T(8,128)(2,1)S(1)} collective-permute-done((bf16[3,80,320]{2,1,0:T(8,128)(2,1)S(1)}, bf16[3,80,320]{2,1,0:T(8,128)(2,1)S(1)}, u32[]{:S(2)}, u32[]{:S(2)}) %collective-permute-start.14) | collective-permute-done | bytes 153632 | tf_op jit(solution)/shard_map/ppermute | solution.py:299
  265.5 1.7 copy.137
  269.1 1.4 collective-permute-done.15
  272.5 1.3 maximum_select_fusion.6
  278.9 1.4 fusion.12
  280.2 1.8 maximum_select_fusion.2
  282.3 1.4 copy.141
  283.8 1.4 copy.142
  (153 shorter events, 40.7 us)
Async XLA Ops:
  0.6 5.3 %copy-start.17 = (bf16[288]{0:T(512)(128)(2,1)S(1)}, bf16[288]{0:T(512)(128)(2,1)}, u32[]{:S(2)}) copy-start(bf16[288]{0:T(512)(128)(2,1)} %param.15) | copy-start | bytes 1732
  0.7 5.3 %copy-start.18 = (bf16[288]{0:T(512)(128)(2,1)S(1)}, bf16[288]{0:T(512)(128)(2,1)}, u32[]{:S(2)}) copy-start(bf16[288]{0:T(512)(128)(2,1)} %param.20) | copy-start | bytes 1732
  0.7 5.4 %copy-start.19 = (s32[4]{0:T(128)S(1)}, s32[4]{0:T(128)}, u32[]{:S(2)}) copy-start(s32[4]{0:T(128)} %param.13) | copy-start | bytes 52
  3.0 23.6 %collective-permute-start.1 = (bf16[288,1536]{1,0:T(8,128)(2,1)}, bf16[288,1536]{1,0:T(8,128)(2,1)S(1)}, u32[]{:S(2)}, u32[]{:S(2)}) collective-permute-start(bf16[288,1536]{1,0:T(8,128)(2,1)} %concatenate.64), channel_id=1, source_target_pairs={{0,1},{1,0},{2,3},{3,2},{4,5},{5,4},{6,7},{7,6},{8,9},{9,8},{10,11... | collective-permute-start | bytes 2654216 | tf_op jit(solution)/shard_map/ppermute | solution.py:299
  6.0 19.9 %collective-permute-start = (bf16[2,288]{1,0:T(2,128)(2,1)S(1)}, bf16[2,288]{1,0:T(2,128)(2,1)S(1)}, u32[]{:S(2)}, u32[]{:S(2)}) collective-permute-start(bf16[2,288]{1,0:T(2,128)(2,1)S(1)} %pad_maximum_fusion.5), channel_id=1, source_target_pairs={{0,1},{1,0},{2,3},{3,2},{4,5},{5,4},{6,7},{7,6},{8,9},{9,8},{10,11... | collective-permute-start | bytes 3464 | tf_op jit(solution)/shard_map/ppermute | solution.py:299
  8.4 3.8 %copy-start.11 = (bf16[1024,576]{0,1:T(8,128)(2,1)S(1)}, bf16[1024,576]{0,1:T(8,128)(2,1)}, u32[]{:S(2)}) copy-start(bf16[1024,576]{0,1:T(8,128)(2,1)} %param.12) | copy-start | bytes 3538948
  10.6 20.6 %copy-start.16 = (s32[1024]{0:T(1024)}, s32[1024]{0:T(1024)S(1)}, u32[]{:S(2)}) copy-start(s32[1024]{0:T(1024)S(1)} %broadcast_select_fusion.5) | copy-start | bytes 12292
  12.2 19.6 %copy-start.12 = (bf16[768,576]{0,1:T(8,128)(2,1)S(1)}, bf16[768,576]{0,1:T(8,128)(2,1)}, u32[]{:S(2)}) copy-start(bf16[768,576]{0,1:T(8,128)(2,1)} %param.23) | copy-start | bytes 2654212
  26.6 7.9 %copy-start.2 = (bf16[288,1536]{1,0:T(8,128)(2,1)S(1)}, bf16[288,1536]{1,0:T(8,128)(2,1)}, u32[]{:S(2)}) copy-start(bf16[288,1536]{1,0:T(8,128)(2,1)} %param.21) | copy-start | bytes 2654212
  26.6 7.9 %copy-start.3 = (bf16[288,1536]{1,0:T(8,128)(2,1)S(1)}, bf16[288,1536]{1,0:T(8,128)(2,1)}, u32[]{:S(2)}) copy-start(bf16[288,1536]{1,0:T(8,128)(2,1)} %param.22) | copy-start | bytes 2654212
  26.6 0.9 copy-start.13
  32.7 33.1 %collective-permute-start.4 = (bf16[384,576]{0,1:T(8,128)(2,1)S(1)}, bf16[384,576]{0,1:T(8,128)(2,1)S(1)}, u32[]{:S(2)}, u32[]{:S(2)}) collective-permute-start(bf16[384,576]{0,1:T(8,128)(2,1)S(1)} %get-tuple-element.126), channel_id=1, source_target_pairs={{0,1},{1,0},{2,3},{3,2},{4,5},{5,4},{6,7},{7,6},{8,9},{9,8},{10,11... | collective-permute-start | bytes 1327112 | tf_op jit(solution)/shard_map/ppermute | solution.py:299
  35.5 31.2 %collective-permute-start.2 = (bf16[288,1536]{1,0:T(8,128)(2,1)}, bf16[288,1536]{1,0:T(8,128)(2,1)S(1)}, u32[]{:S(2)}, u32[]{:S(2)}) collective-permute-start(bf16[288,1536]{1,0:T(8,128)(2,1)} %broadcast_select_fusion), channel_id=1, source_target_pairs={{0,1},{1,0},{2,3},{3,2},{4,5},{5,4},{6,7},{7,6},{8,9},{9,8},{10,11... | collective-permute-start | bytes 2654216 | tf_op jit(solution)/shard_map/ppermute | solution.py:299
  66.7 6.3 %collective-permute-start.5 = (bf16[384,576]{0,1:T(8,128)(2,1)}, bf16[384,576]{0,1:T(8,128)(2,1)}, u32[]{:S(2)}, u32[]{:S(2)}) collective-permute-start(bf16[384,576]{0,1:T(8,128)(2,1)} %broadcast_select_fusion.3), channel_id=1, source_target_pairs={{0,2},{2,0},{4,6},{6,4},{8,10},{10,8},{12,14},{14,12},{16,18},{18,... | collective-permute-start | bytes 1327112 | tf_op jit(solution)/shard_map/ppermute | solution.py:299
  66.7 7.8 %copy-start.5 = (bf16[288,1536]{1,0:T(8,128)(2,1)}, bf16[288,1536]{1,0:T(8,128)(2,1)S(1)}, u32[]{:S(2)}) copy-start(bf16[288,1536]{1,0:T(8,128)(2,1)S(1)} %collective-permute-done.2) | copy-start | bytes 2654212
  67.7 9.2 %collective-permute-start.3 = (bf16[288,1536]{1,0:T(8,128)(2,1)}, bf16[288,1536]{1,0:T(8,128)(2,1)}, u32[]{:S(2)}, u32[]{:S(2)}) collective-permute-start(bf16[288,1536]{1,0:T(8,128)(2,1)} %broadcast_select_fusion.1), channel_id=1, source_target_pairs={{0,2},{2,0},{4,6},{6,4},{8,10},{10,8},{12,14},{14,12},{16,18},{18,... | collective-permute-start | bytes 2654216 | tf_op jit(solution)/shard_map/ppermute | solution.py:299
  72.3 1.7 copy-start.10
  117.5 20.9 %collective-permute-start.7 = (bf16[2,2,448,384]{3,2,1,0:T(8,128)(2,1)}, bf16[2,2,448,384]{3,2,1,0:T(8,128)(2,1)}, u32[]{:S(2)}, u32[]{:S(2)}) collective-permute-start(bf16[2,2,448,384]{3,2,1,0:T(8,128)(2,1)} %dynamic-slice_bitcast_fusion), channel_id=1, source_target_pairs={{0,2},{2,0},{4,6},{6,4},{8,10},{10,8},{12,14},{14,12},{16,18},{18,... | collective-permute-start | bytes 4128776 | tf_op jit(solution)/shard_map/ppermute | solution.py:299
  120.1 23.4 %collective-permute-start.6 = (bf16[2,2,576,384]{3,2,0,1:T(8,128)(2,1)S(1)}, bf16[2,2,576,384]{3,2,0,1:T(8,128)(2,1)}, u32[]{:S(2)}, u32[]{:S(2)}) collective-permute-start(bf16[2,2,576,384]{3,2,0,1:T(8,128)(2,1)S(1)} %bitcast.152), channel_id=1, source_target_pairs={{0,2},{2,0},{4,6},{6,4},{8,10},{10,8},{12,14},{14,12},{16,18},{18,... | collective-permute-start | bytes 5308424 | tf_op jit(solution)/shard_map/ppermute | solution.py:299
  140.7 2.8 copy-start
  141.7 25.2 %collective-permute-start.9 = (bf16[2,448,384]{2,1,0:T(8,128)(2,1)}, bf16[2,448,384]{2,1,0:T(8,128)(2,1)}, u32[]{:S(2)}, u32[]{:S(2)}) collective-permute-start(bf16[2,448,384]{2,1,0:T(8,128)(2,1)} %dynamic-slice_bitcast_fusion.3), channel_id=1, source_target_pairs={{0,4},{2,6},{4,0},{6,2},{8,12},{10,14},{12,8},{14,10},{16,20},{18,... | collective-permute-start | bytes 2064392 | tf_op jit(solution)/shard_map/ppermute | solution.py:299
  147.7 22.6 %collective-permute-start.8 = (bf16[2,576,384]{2,1,0:T(8,128)(2,1)}, bf16[2,576,384]{2,1,0:T(8,128)(2,1)}, u32[]{:S(2)}, u32[]{:S(2)}) collective-permute-start(bf16[2,576,384]{2,1,0:T(8,128)(2,1)} %dynamic-slice_bitcast_fusion.1), channel_id=1, source_target_pairs={{0,1},{1,0},{2,3},{3,2},{4,5},{5,4},{6,7},{7,6},{8,9},{9,8},{10,11... | collective-permute-start | bytes 2654216 | tf_op jit(solution)/shard_map/ppermute | solution.py:299
  149.3 17.7 %copy-start.1 = (bf16[2,2,448,384]{3,2,1,0:T(8,128)(2,1)S(1)}, bf16[2,2,448,384]{3,2,1,0:T(8,128)(2,1)}, u32[]{:S(2)}) copy-start(bf16[2,2,448,384]{3,2,1,0:T(8,128)(2,1)} %copy-done) | copy-start | bytes 4128772
  168.2 0.8 copy-start.6
  169.8 24.3 %collective-permute-start.17 = (bf16[448,384]{1,0:T(8,128)(2,1)}, bf16[448,384]{1,0:T(8,128)(2,1)}, u32[]{:S(2)}, u32[]{:S(2)}) collective-permute-start(bf16[448,384]{1,0:T(8,128)(2,1)} %dynamic-slice_bitcast_fusion.6), channel_id=1, source_target_pairs={{0,1},{1,0},{2,3},{3,2},{4,5},{5,4},{6,7},{7,6},{8,9},{9,8},{10,11... | collective-permute-start | bytes 1032200 | tf_op jit(solution)/shard_map/ppermute | solution.py:299
  172.6 19.1 %copy-start.14 = (bf16[4,2,80,320]{3,2,1,0:T(8,128)(2,1)S(1)}, bf16[4,2,80,320]{3,2,1,0:T(8,128)(2,1)}, u32[]{:S(2)}) copy-start(bf16[4,2,80,320]{3,2,1,0:T(8,128)(2,1)} %get-tuple-element.50) | copy-start | bytes 1228804
  172.7 19.1 %copy-start.15 = (bf16[4,2,80,320]{3,2,1,0:T(8,128)(2,1)S(1)}, bf16[4,2,80,320]{3,2,1,0:T(8,128)(2,1)}, u32[]{:S(2)}) copy-start(bf16[4,2,80,320]{3,2,1,0:T(8,128)(2,1)} %get-tuple-element.51) | copy-start | bytes 1228804
  191.8 2.4 copy-start.7
  194.2 5.2 %copy-start.4 = (bf16[2,576,384]{2,1,0:T(8,128)(2,1)S(1)}, bf16[2,576,384]{2,1,0:T(8,128)(2,1)}, u32[]{:S(2)}) copy-start(bf16[2,576,384]{2,1,0:T(8,128)(2,1)} %fusion.2.after_a_ref) | copy-start | bytes 2654212
  194.2 15.5 %collective-permute-start.10 = (bf16[2,2,3,80,320]{4,3,1,0,2:T(8,128)(2,1)}, bf16[2,2,3,80,320]{4,3,1,0,2:T(8,128)(2,1)S(1)}, u32[]{:S(2)}, u32[]{:S(2)}) collective-permute-start(bf16[2,2,3,80,320]{4,3,1,0,2:T(8,128)(2,1)} %dynamic-slice_bitcast_fusion.2), channel_id=1, source_target_pairs={{0,2},{2,0},{4,6},{6,4},{8,10},{10,8},{12,14},{14,12},{16,18},{18,... | collective-permute-start | bytes 1843208 | tf_op jit(solution)/shard_map/ppermute | solution.py:299
  195.3 10.6 %collective-permute-start.18 = (bf16[448,384]{1,0:T(8,128)(2,1)S(1)}, bf16[448,384]{1,0:T(8,128)(2,1)}, u32[]{:S(2)}, u32[]{:S(2)}) collective-permute-start(bf16[448,384]{1,0:T(8,128)(2,1)S(1)} %fusion.7), channel_id=1, source_target_pairs={{0,8},{2,10},{4,12},{6,14},{8,0},{10,2},{12,4},{14,6},{16,24},{18,... | collective-permute-start | bytes 1032200 | tf_op jit(solution)/shard_map/ppermute | solution.py:299
  200.1 12.5 %collective-permute-start.22 = (bf16[576,384]{1,0:T(8,128)(2,1)}, bf16[576,384]{1,0:T(8,128)(2,1)}, u32[]{:S(2)}, u32[]{:S(2)}) collective-permute-start(bf16[576,384]{1,0:T(8,128)(2,1)} %dynamic-slice_bitcast_fusion.4), channel_id=1, source_target_pairs={{0,4},{2,6},{4,0},{6,2},{8,12},{10,14},{12,8},{14,10},{16,20},{18,... | collective-permute-start | bytes 1327112 | tf_op jit(solution)/shard_map/ppermute | solution.py:299
  207.0 18.0 %collective-permute-start.19 = (bf16[448,384]{1,0:T(8,128)(2,1)S(1)}, bf16[448,384]{1,0:T(8,128)(2,1)S(1)}, u32[]{:S(2)}, u32[]{:S(2)}) collective-permute-start(bf16[448,384]{1,0:T(8,128)(2,1)S(1)} %add_convert_fusion.3), channel_id=1, source_target_pairs={{0,16},{2,18},{4,20},{6,22},{8,24},{10,26},{12,28},{14,30},{16,0},... | collective-permute-start | bytes 1032200 | tf_op jit(solution)/shard_map/ppermute | solution.py:299
  209.9 15.8 %collective-permute-start.11 = (bf16[2,3,80,320]{3,2,0,1:T(8,128)(2,1)S(1)}, bf16[2,3,80,320]{3,2,0,1:T(8,128)(2,1)S(1)}, u32[]{:S(2)}, u32[]{:S(2)}) collective-permute-start(bf16[2,3,80,320]{3,2,0,1:T(8,128)(2,1)S(1)} %dynamic-slice_bitcast_fusion.5), channel_id=1, source_target_pairs={{0,1},{1,0},{2,3},{3,2},{4,5},{5,4},{6,7},{7,6},{8,9},{9,8},{10,11... | collective-permute-start | bytes 921608 | tf_op jit(solution)/shard_map/ppermute | solution.py:299
  213.8 17.7 %collective-permute-start.23 = (bf16[576,384]{1,0:T(8,128)(2,1)S(1)}, bf16[576,384]{1,0:T(8,128)(2,1)S(1)}, u32[]{:S(2)}, u32[]{:S(2)}) collective-permute-start(bf16[576,384]{1,0:T(8,128)(2,1)S(1)} %fusion.5), channel_id=1, source_target_pairs={{0,8},{2,10},{4,12},{6,14},{8,0},{10,2},{12,4},{14,6},{16,24},{18,... | collective-permute-start | bytes 1327112 | tf_op jit(solution)/shard_map/ppermute | solution.py:299
  225.1 14.7 %collective-permute-start.20 = (bf16[448,384]{1,0:T(8,128)(2,1)S(1)}, bf16[448,384]{1,0:T(8,128)(2,1)S(1)}, u32[]{:S(2)}, u32[]{:S(2)}) collective-permute-start(bf16[448,384]{1,0:T(8,128)(2,1)S(1)} %add_convert_fusion.2), channel_id=1, source_target_pairs={{0,4},{2,6},{4,0},{6,2},{8,12},{10,14},{12,8},{14,10},{16,20},{18,... | collective-permute-start | bytes 1032200 | tf_op jit(solution)/shard_map/ppermute | solution.py:299
  225.8 12.2 %collective-permute-start.12 = (bf16[3,80,320]{2,1,0:T(8,128)(2,1)S(1)}, bf16[3,80,320]{2,1,0:T(8,128)(2,1)S(1)}, u32[]{:S(2)}, u32[]{:S(2)}) collective-permute-start(bf16[3,80,320]{2,1,0:T(8,128)(2,1)S(1)} %dynamic-slice_bitcast_fusion.7), channel_id=1, source_target_pairs={{0,4},{2,6},{4,0},{6,2},{8,12},{10,14},{12,8},{14,10},{16,20},{18,... | collective-permute-start | bytes 460808 | tf_op jit(solution)/shard_map/ppermute | solution.py:299
  231.7 23.8 %collective-permute-start.24 = (bf16[576,384]{1,0:T(8,128)(2,1)S(1)}, bf16[576,384]{1,0:T(8,128)(2,1)S(1)}, u32[]{:S(2)}, u32[]{:S(2)}) collective-permute-start(bf16[576,384]{1,0:T(8,128)(2,1)S(1)} %add_convert_fusion.1), channel_id=1, source_target_pairs={{0,16},{2,18},{4,20},{6,22},{8,24},{10,26},{12,28},{14,30},{16,0},... | collective-permute-start | bytes 1327112 | tf_op jit(solution)/shard_map/ppermute | solution.py:299
  238.0 7.3 %collective-permute-start.13 = (bf16[3,80,320]{2,1,0:T(8,128)(2,1)S(1)}, bf16[3,80,320]{2,1,0:T(8,128)(2,1)S(1)}, u32[]{:S(2)}, u32[]{:S(2)}) collective-permute-start(bf16[3,80,320]{2,1,0:T(8,128)(2,1)S(1)} %fusion.8), channel_id=1, source_target_pairs={{0,8},{2,10},{4,12},{6,14},{8,0},{10,2},{12,4},{14,6},{16,24},{18,... | collective-permute-start | bytes 460808 | tf_op jit(solution)/shard_map/ppermute | solution.py:299
  240.0 24.0 %collective-permute-start.21 = (bf16[2,448,384]{2,1,0:T(8,128)(2,1)S(1)}, bf16[2,448,384]{2,1,0:T(8,128)(2,1)S(1)}, u32[]{:S(2)}, u32[]{:S(2)}) collective-permute-start(bf16[2,448,384]{2,1,0:T(8,128)(2,1)S(1)} %maximum_select_fusion.10), channel_id=1, source_target_pairs={{0,2},{2,0},{4,6},{6,4},{8,10},{10,8},{12,14},{14,12},{16,18},{18,... | collective-permute-start | bytes 2064392 | tf_op jit(solution)/shard_map/ppermute | solution.py:299
  245.4 18.0 %collective-permute-start.14 = (bf16[3,80,320]{2,1,0:T(8,128)(2,1)S(1)}, bf16[3,80,320]{2,1,0:T(8,128)(2,1)S(1)}, u32[]{:S(2)}, u32[]{:S(2)}) collective-permute-start(bf16[3,80,320]{2,1,0:T(8,128)(2,1)S(1)} %add_convert_fusion.5), channel_id=1, source_target_pairs={{0,16},{2,18},{4,20},{6,22},{8,24},{10,26},{12,28},{14,30},{16,0},... | collective-permute-start | bytes 460808 | tf_op jit(solution)/shard_map/ppermute | solution.py:299
  255.6 15.2 %collective-permute-start.25 = (bf16[576,384]{1,0:T(8,128)(2,1)S(1)}, bf16[576,384]{1,0:T(8,128)(2,1)S(1)}, u32[]{:S(2)}, u32[]{:S(2)}) collective-permute-start(bf16[576,384]{1,0:T(8,128)(2,1)S(1)} %add_convert_fusion), channel_id=1, source_target_pairs={{0,4},{2,6},{4,0},{6,2},{8,12},{10,14},{12,8},{14,10},{16,20},{18,... | collective-permute-start | bytes 1327112 | tf_op jit(solution)/shard_map/ppermute | solution.py:299
  263.4 7.1 %collective-permute-start.15 = (bf16[3,80,320]{2,1,0:T(8,128)(2,1)S(1)}, bf16[3,80,320]{2,1,0:T(8,128)(2,1)S(1)}, u32[]{:S(2)}, u32[]{:S(2)}) collective-permute-start(bf16[3,80,320]{2,1,0:T(8,128)(2,1)S(1)} %add_convert_fusion.4), channel_id=1, source_target_pairs={{0,4},{2,6},{4,0},{6,2},{8,12},{10,14},{12,8},{14,10},{16,20},{18,... | collective-permute-start | bytes 460808 | tf_op jit(solution)/shard_map/ppermute | solution.py:299
  270.7 3.1 %collective-permute-start.16 = (bf16[2,3,80,320]{3,2,1,0:T(8,128)(2,1)S(1)}, bf16[2,3,80,320]{3,2,1,0:T(8,128)(2,1)S(1)}, u32[]{:S(2)}, u32[]{:S(2)}) collective-permute-start(bf16[2,3,80,320]{3,2,1,0:T(8,128)(2,1)S(1)} %maximum_select_fusion.12), channel_id=1, source_target_pairs={{0,2},{2,0},{4,6},{6,4},{8,10},{10,8},{12,14},{14,12},{16,18},{18,... | collective-permute-start | bytes 921608 | tf_op jit(solution)/shard_map/ppermute | solution.py:299
  270.9 1.6 copy-start.9
  272.0 8.3 %collective-permute-start.26 = (bf16[2,576,384]{2,1,0:T(8,128)(2,1)}, bf16[2,576,384]{2,1,0:T(8,128)(2,1)}, u32[]{:S(2)}, u32[]{:S(2)}) collective-permute-start(bf16[2,576,384]{2,1,0:T(8,128)(2,1)} %maximum_select_fusion.7), channel_id=1, source_target_pairs={{0,2},{2,0},{4,6},{6,4},{8,10},{10,8},{12,14},{14,12},{16,18},{18,... | collective-permute-start | bytes 2654216 | tf_op jit(solution)/shard_map/ppermute | solution.py:299
  274.1 0.9 copy-start.8
